TPU v7x, 256 devices: a whole 4x4x8 slice. The times are simulated.
256 devices in a mesh: role: 2 (over x_lo), dev: 64 (over y, x_hi, z), cores: 2 (over core).
Axes of the slice: x: 4 (x_hi: 2, x_lo: 2; x = x_hi * 2 + x_lo), y: 4, z: 8, core: 2. Of those that a mesh axis runs over, the one named last changes fastest.
Arguments:
- tokens: bfloat16 [4096, 3584], P(('role', 'dev', 'cores')), may hold values from -6 to 6
- norm_gain: float32 [3584], replicated, may hold values from 0.1 to 1.9
- routes: int32 [4096, 8], P(('role', 'dev', 'cores')), may hold values from 0 to 127, all different within a row; in each aligned block of 16 rows (0 to 15, 16 to 31, ...) at most 2 rows name the same one
- route_weight: float32 [4096, 8], P(('role', 'dev', 'cores')), may hold values from 0.05 to 0.35
- w_gate: bfloat16 [128, 3584, 1024], P(('role', 'dev'), None, 'cores'), may hold values from -0.09375 to 0.09375
- w_up: bfloat16 [128, 3584, 1024], P(('role', 'dev'), None, 'cores'), may hold values from -0.09375 to 0.09375
- w_down: bfloat16 [128, 1024, 3584], P(('role', 'dev'), 'cores'), may hold values from -0.1875 to 0.1875
- query_latent: bfloat16 [1024, 128, 512], P(('role', 'dev', 'cores')), may hold values from -21 to 21
- query_rope: bfloat16 [1024, 128, 64], P(('role', 'dev', 'cores')), may hold values from -6 to 6
- cache_latent: bfloat16 [1024, 256, 512], P(('role', 'dev', 'cores')), may hold values from -6 to 6
- cache_rope: bfloat16 [1024, 64, 256], P(('role', 'dev', 'cores')), may hold values from -6 to 6
- lengths: int32 [1024], P(('role', 'dev', 'cores')), may hold values from 1 to 256, 131072 in all
Outputs:
- layer_out: bfloat16 [4096, 3584], P(('role', 'dev', 'cores'))
- attention_latent: bfloat16 [1024, 128, 512], P(('role', 'dev', 'cores'))
Inputs may be any that keep to these rules, and one draw needn't show every extreme that they name: `routes`: each token names 8 different experts; at most 2 of the 16 tokens of one device name the same expert.
All inputs are finite; a program needn't handle non-finite values. No bound on the sum of `lengths` on one device may be relied on, other than what follows from the above.
Results may differ from a plain program's by a relative error of at most 0.0048.
Values may be sent and summed in bfloat16 or wider, within the bound.
No kernel may reach another device: no remote copies, remote signals or barrier semaphores. Data moves between devices by JAX's collectives and lax.ppermute only.
A program may use at most 128 MiB of HBM per device.

v0:
```python
import jax
import jax.numpy as jnp
from jax import lax
from jax.sharding import PartitionSpec as P

score_scale = 192.0 ** (-0.5)
epsilon = 1e-06


def per_device(
    tokens,
    norm_gain,
    routes,
    route_weight,
    w_gate,
    w_up,
    w_down,
    query_latent,
    query_rope,
    cache_latent,
    cache_rope,
    lengths,
):
    groups = lax.axis_size(("role", "dev"))
    token_count = tokens.shape[0]
    top_count = routes.shape[1]
    model_width = tokens.shape[1]
    capacity = max(2, token_count * top_count * 2 // groups)
    slot_count = groups * capacity
    widened = tokens.astype(jnp.float32)
    inverse = lax.rsqrt(jnp.mean(widened * widened, axis=-1, keepdims=True) + epsilon)
    normed = (widened * inverse * norm_gain).astype(jnp.bfloat16)
    flat_routes = routes.reshape(-1)
    onehot = (flat_routes[:, None] == jnp.arange(groups, dtype=jnp.int32)[None, :]).astype(
        jnp.int32
    )
    slot_rank = jnp.sum((jnp.cumsum(onehot, axis=0) - 1) * onehot, axis=1)
    target = flat_routes * capacity + slot_rank
    route_place = (target[:, None] == jnp.arange(slot_count, dtype=jnp.int32)[None, :]).astype(
        jnp.bfloat16
    )
    token_place = jnp.sum(route_place.reshape(token_count, top_count, slot_count), axis=1)
    outgoing = lax.dot_general(
        token_place, normed, (((0,), (0,)), ((), ())), preferred_element_type=jnp.float32
    )
    outgoing = outgoing.astype(jnp.bfloat16).reshape(groups, capacity, model_width)
    arrived = lax.all_to_all(outgoing, ("role", "dev"), split_axis=0, concat_axis=0, tiled=True)
    arrived = arrived.reshape(slot_count, model_width)
    both_cores = lax.all_gather(arrived, "cores", axis=0, tiled=True)
    gate_proj = jnp.dot(both_cores, w_gate[0], preferred_element_type=jnp.float32)
    up_proj = jnp.dot(both_cores, w_up[0], preferred_element_type=jnp.float32)
    hidden = (jax.nn.silu(gate_proj) * up_proj).astype(jnp.bfloat16)
    partial_value = jnp.dot(hidden, w_down[0], preferred_element_type=jnp.float32)
    rounded = lax.optimization_barrier(partial_value.astype(jnp.bfloat16)).astype(jnp.float32)
    results = lax.psum_scatter(
        rounded.astype(jnp.bfloat16), "cores", scatter_dimension=0, tiled=True
    )
    returned = lax.all_to_all(
        results.reshape(groups, capacity, model_width),
        ("role", "dev"),
        split_axis=0,
        concat_axis=0,
        tiled=True,
    )
    returned = returned.reshape(slot_count, model_width)
    picked = jnp.dot(route_place, returned, preferred_element_type=jnp.float32)
    combined = jnp.sum(
        picked.reshape(token_count, top_count, model_width) * route_weight[:, :, None], axis=1
    )
    layer_out = (widened + combined).astype(jnp.bfloat16)
    scores = jnp.einsum(
        "rhl,rpl->rhp", query_latent, cache_latent, preferred_element_type=jnp.float32
    )
    scores = (
        scores
        + jnp.einsum("rhk,rkp->rhp", query_rope, cache_rope, preferred_element_type=jnp.float32)
    ) * score_scale
    in_range = jnp.arange(cache_latent.shape[1], dtype=jnp.int32)[None, :] < lengths[:, None]
    scores = jnp.where(in_range[:, None, :], scores, -1e30)
    highest = jnp.max(scores, axis=2, keepdims=True)
    weights = jnp.exp(scores - highest)
    probabilities = (weights / jnp.sum(weights, axis=2, keepdims=True)).astype(jnp.bfloat16)
    attention_latent = jnp.einsum(
        "rhp,rpl->rhl", probabilities, cache_latent, preferred_element_type=jnp.float32
    ).astype(jnp.bfloat16)
    return (layer_out, attention_latent)


def solution(mesh):
    return jax.shard_map(
        per_device,
        mesh=mesh,
        in_specs=(
            P(("role", "dev", "cores"), None),
            P(),
            P(("role", "dev", "cores"), None),
            P(("role", "dev", "cores"), None),
            P(("role", "dev"), None, "cores"),
            P(("role", "dev"), None, "cores"),
            P(("role", "dev"), "cores", None),
            P(("role", "dev", "cores"), None, None),
            P(("role", "dev", "cores"), None, None),
            P(("role", "dev", "cores"), None, None),
            P(("role", "dev", "cores"), None, None),
            P(("role", "dev", "cores")),
        ),
        out_specs=(P(("role", "dev", "cores"), None), P(("role", "dev", "cores"), None, None)),
        check_vma=False,
    )
```

profile of v0, /device:TPU:6, one launch (start us, length us, event | category | flops | bytes accessed | tf_op | source)
XLA Modules:
  0.0 206.9 jit_solution(1256810507250776066)
XLA Ops:
  7.2 0.8 copy.20
  8.2 0.1 fusion.33
  8.2 0.2 reduce_window_sum.11
  8.4 0.2 select_reduce_fusion
  8.7 0.1 fusion.31
  8.8 1.0 fusion.21
  9.9 2.8 %convolution_convert_fusion.1 = bf16[256,3584]{1,0:T(8,128)(2,1)} fusion(bf16[16,256]{1,0:T(8,128)(2,1)S(1)} %fusion.31, bf16[16,3584]{1,0:T(8,128)(2,1)} %param.12, f32[3584]{0:T(1024)} %param.13, f32[16]{0:T(128)S(1)} %add_rsqrt_fusion), kind=kOutput, calls=%fused_computation.2 | convolution fusion | flops 30507008 | bytes 1972288 | tf_op jit(solution)/shard_map/dot_general | solution.py:43
  12.7 3.9 %reshape.88 = bf16[128,2,3584]{2,1,0:T(2,128)(2,1)S(1)} reshape(bf16[256,3584]{1,0:T(8,128)(2,1)} %convolution_convert_fusion.1) | data formatting | bytes 3670016 | tf_op jit(solution)/shard_map/reshape | solution.py:46
  16.6 60.8 %all_to_all.10 = bf16[128,2,3584]{2,1,0:T(2,128)(2,1)} all-to-all(bf16[128,2,3584]{2,1,0:T(2,128)(2,1)S(1)} %reshape.88), channel_id=1, replica_groups=mesh['role'=2,'dev'=64,'cores'=2] {'role','dev'}, dimensions={0} | all-to-all | bytes 3670016 | tf_op jit(solution)/shard_map/all_to_all | solution.py:47
  77.4 4.9 %reshape.89 = bf16[256,3584]{1,0:T(8,128)(2,1)} reshape(bf16[128,2,3584]{2,1,0:T(2,128)(2,1)} %all_to_all.10) | data formatting | bytes 3670016 | tf_op jit(solution)/shard_map/reshape | solution.py:48
  82.4 14.8 %all-gather.2.cloned.1.call-done = bf16[512,3584]{1,0:T(8,128)(2,1)} async-done(((bf16[256,3584]{1,0:T(8,128)(2,1)}), bf16[512,3584]{1,0:T(8,128)(2,1)}) %all-gather.2.cloned.1.call-update) | async-done | bytes 3670032 | tf_op jit(solution)/shard_map/all_gather | solution.py:49
  97.2 5.2 %fusion.4 = f32[512,512]{1,0:T(8,128)S(1)} fusion(bf16[512,3584]{1,0:T(8,128)(2,1)} %all-gather.2.cloned.1.call-done, bf16[1,3584,512]{2,1,0:T(8,128)(2,1)} %param.16), kind=kOutput, calls=%fused_computation.7 | convolution fusion | flops 1879048192 | bytes 8388608 | tf_op jit(solution)/shard_map/dot_general | solution.py:50
  102.4 10.1 %convolution_convert_fusion = bf16[512,3584]{1,0:T(8,128)(2,1)} fusion(bf16[1,512,3584]{2,1,0:T(8,128)(2,1)} %param.18, bf16[512,3584]{1,0:T(8,128)(2,1)} %all-gather.2.cloned.1.call-done, bf16[1,3584,512]{2,1,0:T(8,128)(2,1)} %param.17, f32[512,512]{1,0:T(8,128)S(1)} %fusion.4), kind=kOutput, calls=%fused_computation.1 | convolution fusion | flops 3761504256 | bytes 15728640 | tf_op jit(solution)/shard_map/dot_general | solution.py:53
  112.6 18.3 %reduce-scatter.2.cloned.1.call-done = bf16[256,3584]{1,0:T(8,128)(2,1)} async-done(((bf16[512,3584]{1,0:T(8,128)(2,1)}), bf16[256,3584]{1,0:T(8,128)(2,1)}) %reduce-scatter.2.cloned.1.call-update) | async-done | bytes 1835024 | tf_op jit(solution)/shard_map/reduce_scatter | solution.py:55
  130.8 4.7 %reshape.90 = bf16[128,2,3584]{2,1,0:T(2,128)(2,1)} reshape(bf16[256,3584]{1,0:T(8,128)(2,1)} %reduce-scatter.2.cloned.1.call-done) | data formatting | bytes 3670016 | tf_op jit(solution)/shard_map/reshape | solution.py:59
  135.5 14.1 %all-to-all-start.1 = ((bf16[128,2,3584]{2,1,0:T(2,128)(2,1)}), bf16[128,2,3584]{2,1,0:T(2,128)(2,1)S(1)}, u32[]{:S(2)}, u32[]{:S(2)}) async-start(bf16[128,2,3584]{2,1,0:T(2,128)(2,1)} %reshape.90), calls=%async_computation.2 | async-start | bytes 3670016 | tf_op jit(solution)/shard_map/all_to_all | solution.py:58
  149.9 0.3 fusion.37
  150.1 1.5 fusion.15
  151.7 0.2 fusion.36
  151.9 1.8 convolution_convert_fusion.2
  153.7 41.7 %all-to-all-done.1 = bf16[128,2,3584]{2,1,0:T(2,128)(2,1)S(1)} async-done(((bf16[128,2,3584]{2,1,0:T(2,128)(2,1)}), bf16[128,2,3584]{2,1,0:T(2,128)(2,1)S(1)}, u32[]{:S(2)}, u32[]{:S(2)}) %all-to-all-start.1) | async-done | bytes 1835040 | tf_op jit(solution)/shard_map/all_to_all | solution.py:58
  195.4 1.7 reshape.92
  197.1 2.3 %fusion.9 = f32[16,3584]{1,0:T(8,128)S(1)} fusion(bf16[256,3584,1]{1,0,2:T(8,128)(2,1)} %reshape.92, f32[16,8]{1,0:T(8,128)S(1)} %copy.22, s32[16,8]{1,0:T(8,128)S(1)} %multiply_add_fusion), kind=kOutput, calls=%fused_computation.10 | convolution fusion | flops 235773952 | bytes 2065408 | tf_op jit(solution)/shard_map/dot_general | solution.py:66
  199.4 0.7 fusion.24
  (22 shorter events, 0.5 us)
Async XLA Ops:
  7.2 143.0 %copy-start = (bf16[4,256,512]{2,1,0:T(8,128)(2,1)S(1)}, bf16[4,256,512]{2,1,0:T(8,128)(2,1)}, u32[]{:S(2)}) copy-start(bf16[4,256,512]{2,1,0:T(8,128)(2,1)} %param.21) | copy-start | bytes 3145732
  7.2 90.0 %all-gather.2.cloned.1.call-start = ((), (), s32[]{:S(2)}) async-start(), calls=%async_computation.3 | async-start | bytes 5505024 | tf_op jit(solution)/shard_map/all_gather | solution.py:49
  82.3 48.5 %reduce-scatter.2.cloned.1.call-start = ((), (), s32[]{:S(2)}) async-start(), calls=%async_computation.4 | async-start | bytes 5505024 | tf_op jit(solution)/shard_map/reduce_scatter | solution.py:55
  112.5 37.2 %copy-start.4 = (f32[16,8]{0,1:T(8,128)S(1)}, f32[16,8]{0,1:T(8,128)}, u32[]{:S(2)}) copy-start(f32[16,8]{0,1:T(8,128)} %param.15) | copy-start | bytes 1540
  112.5 37.3 %copy-start.5 = (s32[4]{0:T(128)S(1)}, s32[4]{0:T(128)}, u32[]{:S(2)}) copy-start(s32[4]{0:T(128)} %param.23) | copy-start | bytes 52
  112.5 37.3 %copy-start.2 = (bf16[4,64,256]{2,1,0:T(8,128)(2,1)S(1)}, bf16[4,64,256]{2,1,0:T(8,128)(2,1)}, u32[]{:S(2)}) copy-start(bf16[4,64,256]{2,1,0:T(8,128)(2,1)} %param.22) | copy-start | bytes 393220
  112.5 37.3 %copy-start.3 = (bf16[4,128,64]{1,2,0:T(8,128)(2,1)S(1)}, bf16[4,128,64]{1,2,0:T(8,128)(2,1)}, u32[]{:S(2)}) copy-start(bf16[4,128,64]{1,2,0:T(8,128)(2,1)} %param.20) | copy-start | bytes 196612
  135.5 59.9 %all-to-all-start.1 = ((bf16[128,2,3584]{2,1,0:T(2,128)(2,1)}), bf16[128,2,3584]{2,1,0:T(2,128)(2,1)S(1)}, u32[]{:S(2)}, u32[]{:S(2)}) async-start(bf16[128,2,3584]{2,1,0:T(2,128)(2,1)} %reshape.90), calls=%async_computation.2 | async-start | bytes 3670016 | tf_op jit(solution)/shard_map/all_to_all | solution.py:58
  153.7 45.6 %copy-start.1 = (bf16[16,3584]{1,0:T(8,128)(2,1)S(1)}, bf16[16,3584]{1,0:T(8,128)(2,1)}, u32[]{:S(2)}) copy-start(bf16[16,3584]{1,0:T(8,128)(2,1)} %param.12) | copy-start | bytes 344068
Sparse Core Ops, SparseCore 0:
  82.5 14.6 all-gather.1
  112.6 18.1 reduce-scatter.1
where the time goes:
time: 210 us; the launch traced here: 207 us
  waiting for transfers between devices  74.8 us (36%)
  blocking collectives  60.8 us (29%)
  matrix products  24 us (11%)
  local copies, waits for them, and re-layouts  16.3 us (8%)
  starting transfers between devices  14.2 us (7%)
  between operations  14.2 us (7%)
  other arithmetic  2.62 us (1%)
    all_to_all x1, blocking collectives, per_device(): lax.all_to_all(outgoing, ('role', 'dev'), split_axis=0, concat_axis=0, ti...  60.8 us
    all_to_all x1, waiting for transfers between devices, per_device(): lax.all_to_all(results.reshape(groups, capacity, model_width), ('role', '...  41.7 us
    reduce_scatter x1, waiting for transfers between devices, per_device(): lax.psum_scatter(rounded.astype(jnp.bfloat16), 'cores', scatter_dimension...  18.3 us
    all_gather x1, waiting for transfers between devices, per_device(): both_cores = lax.all_gather(arrived, 'cores', axis=0, tiled=True)  14.8 us
    all_to_all x1, starting transfers between devices, per_device(): lax.all_to_all(results.reshape(groups, capacity, model_width), ('role', '...  14.1 us
    dot_general x1, matrix products, per_device(): jnp.dot(hidden, w_down[0], preferred_element_type=jnp.float32)  10.1 us
    dot_general x1, matrix products, per_device(): jnp.dot(both_cores, w_gate[0], preferred_element_type=jnp.float32)  5.21 us
    reshape x1, local copies, waits for them, and re-layouts, per_device(): arrived = arrived.reshape(slot_count, model_width)  4.92 us
  transfers between devices with their start and end apart: 3, of which 3 were waited for; matrix products, arithmetic and copies ran while one was open for 2% of the time, Pallas kernels for 0%

commit v1 on v0

v1 whole, which is shorter than its diff:
```python
import functools
import jax
import jax.numpy as jnp
from jax import lax
from jax.experimental import pallas as pl
from jax.experimental.pallas import tpu as pltpu
from jax.sharding import Mesh, PartitionSpec as P

score_scale = 192.0 ** (-0.5)
epsilon = 1e-06
PLANE = ("xl", "y", "xh")
EXPERT = ("xl", "y", "xh", "z")
ALL = ("xl", "y", "xh", "z", "c")
TAIL = 128
VMEM_LIMIT = 56 * 1024 * 1024


def attention(query_latent, query_rope, cache_latent, cache_rope, lengths):
    scores = jnp.einsum(
        "rhl,rpl->rhp", query_latent, cache_latent, preferred_element_type=jnp.float32
    )
    scores = (
        scores
        + jnp.einsum("rhk,rkp->rhp", query_rope, cache_rope, preferred_element_type=jnp.float32)
    ) * score_scale
    in_range = jnp.arange(cache_latent.shape[1], dtype=jnp.int32)[None, :] < lengths[:, None]
    scores = jnp.where(in_range[:, None, :], scores, -1e30)
    highest = jnp.max(scores, axis=2, keepdims=True)
    weights = jnp.exp(scores - highest)
    probabilities = (weights / jnp.sum(weights, axis=2, keepdims=True)).astype(jnp.bfloat16)
    return jnp.einsum(
        "rhp,rpl->rhl", probabilities, cache_latent, preferred_element_type=jnp.float32
    ).astype(jnp.bfloat16)


def call(kernel, out_shape, *operands, flops=0, scratch=()):
    moved = sum(x.size * x.dtype.itemsize for x in operands) + sum(
        x.size * x.dtype.itemsize for x in jax.tree.leaves(out_shape)
    )
    return pl.pallas_call(
        kernel,
        out_shape=out_shape,
        scratch_shapes=scratch,
        compiler_params=pltpu.CompilerParams(vmem_limit_bytes=VMEM_LIMIT),
        cost_estimate=pl.CostEstimate(flops=flops, bytes_accessed=moved, transcendentals=0),
    )(*operands)


def shape(*dims, dtype=jnp.bfloat16):
    return jax.ShapeDtypeStruct(dims, dtype)


def norm_kernel(tokens, gain, tail, packed):
    width = tokens.shape[1]
    widened = tokens[...].astype(jnp.float32)
    inverse = lax.rsqrt(jnp.mean(widened * widened, axis=1, keepdims=True) + epsilon)
    packed[:, :width] = (widened * inverse * gain[...]).astype(jnp.bfloat16)
    packed[:, width:] = tail[...]


def dispatch_kernel(top, own, *refs):
    blocks, (outgoing, scale) = refs[:-2], refs[-2:]
    count = blocks[0].shape[0]
    gathered = count * len(blocks)
    places = own.shape[1]
    width = outgoing.shape[1]
    info = jnp.concatenate([b[:, width:] for b in blocks], axis=0).astype(jnp.float32)
    experts = own[...]
    names = jnp.zeros((gathered, places), jnp.float32)
    weight = jnp.zeros((gathered, places), jnp.float32)
    for k in range(top):
        match = info[:, k : k + 1] == experts
        share = (
            info[:, top + k : top + k + 1]
            + info[:, 2 * top + k : 2 * top + k + 1]
            + info[:, 3 * top + k : 3 * top + k + 1]
        )
        names = jnp.where(match, 1.0, names)
        weight = weight + jnp.where(match, share, 0.0)
    row = lax.broadcasted_iota(jnp.int32, (gathered, gathered), 0)
    column = lax.broadcasted_iota(jnp.int32, (gathered, gathered), 1)
    before = jnp.where((column < row) & (column // count == row // count), 1.0, 0.0)
    rank = jnp.dot(
        before.astype(jnp.bfloat16), names.astype(jnp.bfloat16), preferred_element_type=jnp.float32
    )
    token = lax.broadcasted_iota(jnp.int32, (gathered, places), 0)
    slot = lax.broadcasted_iota(jnp.int32, (gathered, places), 1) % (2 * len(blocks))
    here = (names > 0.0) & ((token // count) * 2 + rank.astype(jnp.int32) == slot)
    scale[...] = jnp.where(here, weight, 0.0)
    place = jnp.where(here, 1.0, 0.0).astype(jnp.bfloat16)
    step = 512
    for start in range(0, width, step):
        rows = jnp.concatenate([b[:, start : start + step] for b in blocks], axis=0)
        outgoing[:, start : start + step] = lax.dot_general(
            place, rows, (((0,), (0,)), ((), ())), preferred_element_type=jnp.float32
        ).astype(jnp.bfloat16)


def combine_kernel(scale, returned, *blocks):
    count = blocks[0].shape[0]
    width = returned.shape[1]
    high = scale[...].astype(jnp.bfloat16)
    low = (scale[...] - high.astype(jnp.float32)).astype(jnp.bfloat16)
    step = 512
    for start in range(0, width, step):
        rows = returned[:, start : start + step]
        sums = jnp.dot(high, rows, preferred_element_type=jnp.float32) + jnp.dot(
            low, rows, preferred_element_type=jnp.float32
        )
        for i, block in enumerate(blocks):
            block[:, start : start + step] = sums[i * count : (i + 1) * count].astype(block.dtype)


def add_kernel(up2, up3, across, down2, down3, new_up2, new_down2):
    f32 = jnp.float32
    new_up2[...] = (
        up2[...].astype(f32) + up3[...].astype(f32) + across[...].astype(f32)
    ).astype(jnp.bfloat16)
    new_down2[...] = (down2[...].astype(f32) + down3[...].astype(f32)).astype(jnp.bfloat16)


def final_kernel(tokens, own, *refs):
    total = own[...]
    for part in refs[:-1]:
        total = total + part[...].astype(jnp.float32)
    refs[-1][...] = (tokens[...].astype(jnp.float32) + total).astype(jnp.bfloat16)


def expert_kernel(rows, *refs):
    weights, out, buffers, sems, total = refs[:6], refs[6], refs[7:13], refs[13], refs[14]
    tile = 256
    tiles = weights[0].shape[1] // tile
    copies = []
    for half in range(2):
        for t in range(tiles):
            group = []
            for m in range(3):
                cut = pl.ds(t * tile, tile)
                at = (cut, slice(None)) if m == 2 else (slice(None), cut)
                index = half * 3 + m
                copy = pltpu.make_async_copy(
                    weights[index].at[at], buffers[index].at[at], sems.at[index, t]
                )
                copy.start()
                group.append(copy)
            copies.append(group)
    x = rows[...]
    step = 512
    width = out.shape[1]
    for half in range(2):
        gate_buffer, up_buffer, down_buffer = buffers[half * 3 : half * 3 + 3]
        hidden = []
        for t in range(tiles):
            group = copies[half * tiles + t]
            cut = slice(t * tile, (t + 1) * tile)
            group[0].wait()
            gate = jnp.dot(x, gate_buffer[:, cut], preferred_element_type=jnp.float32)
            group[1].wait()
            up = jnp.dot(x, up_buffer[:, cut], preferred_element_type=jnp.float32)
            hidden.append((gate / (1.0 + jnp.exp(-gate)) * up).astype(jnp.bfloat16))
        for t in range(tiles):
            copies[half * tiles + t][2].wait()
        activation = jnp.concatenate(hidden, axis=1)
        for start in range(0, width, step):
            cut = slice(start, start + step)
            partial = jnp.dot(
                activation, down_buffer[:, cut], preferred_element_type=jnp.float32
            ).astype(jnp.bfloat16)
            if half == 0:
                total[:, cut] = partial
            else:
                out[:, cut] = (
                    total[:, cut].astype(jnp.float32) + partial.astype(jnp.float32)
                ).astype(jnp.bfloat16)


def experts(rows, weights):
    count, width = rows.shape
    any_space = pl.BlockSpec(memory_space=pl.ANY)
    flops = 2 * count * sum(w.size for w in weights)
    return pl.pallas_call(
        expert_kernel,
        out_shape=shape(count, width),
        in_specs=[pl.BlockSpec(memory_space=pltpu.VMEM)] + [any_space] * 6,
        out_specs=pl.BlockSpec(memory_space=pltpu.VMEM),
        scratch_shapes=[pltpu.VMEM(w.shape, w.dtype) for w in weights]
        + [pltpu.SemaphoreType.DMA((6, 2)), pltpu.VMEM((count, width), jnp.bfloat16)],
        compiler_params=pltpu.CompilerParams(vmem_limit_bytes=VMEM_LIMIT),
        cost_estimate=pl.CostEstimate(
            flops=flops, bytes_accessed=2 * sum(w.size for w in weights), transcendentals=0
        ),
    )(rows, *weights)


def from_line(rows, distance):
    planes = lax.axis_size("z")
    return lax.ppermute(rows, "z", [((i + distance) % planes, i) for i in range(planes)])


def per_device(
    tokens,
    norm_gain,
    routes,
    route_weight,
    w_gate,
    w_up,
    w_down,
    query_latent,
    query_rope,
    cache_latent,
    cache_rope,
    lengths,
):
    planes = lax.axis_size("z")
    places = lax.axis_size(PLANE)
    count, top = routes.shape
    width = tokens.shape[1]
    gathered = planes * count
    slots = 2 * planes

    high = route_weight.astype(jnp.bfloat16)
    rest = route_weight - high.astype(jnp.float32)
    middle = rest.astype(jnp.bfloat16)
    low = (rest - middle.astype(jnp.float32)).astype(jnp.bfloat16)
    tail = jnp.concatenate([routes.astype(jnp.bfloat16), high, middle, low], axis=1)
    tail = jnp.pad(tail, ((0, 0), (0, TAIL - 4 * top)))
    packed = call(norm_kernel, shape(count, width + TAIL), tokens, norm_gain[None], tail)

    up2, down2 = from_line(packed, 2), from_line(packed, -2)
    up1, down1 = from_line(packed, 1), from_line(packed, -1)
    across, up3, down3 = from_line(up2, 2), from_line(up2, 1), from_line(down2, -1)

    own = (
        (jnp.arange(places * slots, dtype=jnp.int32) // slots) * planes + lax.axis_index("z")
    ).astype(jnp.float32)[None]
    outgoing, scale = call(
        functools.partial(dispatch_kernel, top),
        (shape(places * slots, width), shape(gathered, places * slots, dtype=jnp.float32)),
        own,
        packed,
        up1,
        up2,
        up3,
        across,
        down3,
        down2,
        down1,
    )
    weights = (w_gate[0], w_up[0], w_down[0])
    *held, outgoing = lax.optimization_barrier((*weights, outgoing))
    far = [lax.ppermute(w, "c", [(0, 1), (1, 0)]) for w in held]
    arrived = lax.all_to_all(outgoing, PLANE, split_axis=0, concat_axis=0, tiled=True)
    result = experts(arrived, (*weights, *far))
    returned = lax.all_to_all(result, PLANE, split_axis=0, concat_axis=0, tiled=True)
    own, up1, up2, up3, across, down3, down2, down1 = call(
        combine_kernel,
        (shape(count, width, dtype=jnp.float32),) + (shape(count, width),) * (planes - 1),
        scale,
        returned,
    )
    across, up3, down3 = from_line(across, -2), from_line(up3, -1), from_line(down3, 1)
    up1, down1 = from_line(up1, -1), from_line(down1, 1)
    up2, down2 = call(
        add_kernel, (shape(count, width),) * 2, up2, up3, across, down2, down3
    )
    up2, down2 = from_line(up2, -2), from_line(down2, 2)
    layer_out = call(final_kernel, shape(count, width), tokens, own, up1, down1, up2, down2)
    return layer_out, attention(query_latent, query_rope, cache_latent, cache_rope, lengths)


def solution(mesh):
    split = Mesh(mesh.devices.reshape(2, 4, 2, 8, 2), ALL)
    return jax.shard_map(
        per_device,
        mesh=split,
        in_specs=(
            P(ALL, None),
            P(),
            P(ALL, None),
            P(ALL, None),
            P(EXPERT, None, "c"),
            P(EXPERT, None, "c"),
            P(EXPERT, "c", None),
            P(ALL, None, None),
            P(ALL, None, None),
            P(ALL, None, None),
            P(ALL, None, None),
            P(ALL),
        ),
        out_specs=(P(ALL, None), P(ALL, None, None)),
        check_vma=False,
    )
```

time: 210 us -> 147 us (0.70)
  waiting for transfers between devices: 74.8 us -> 37.1 us
  blocking collectives: 60.8 us -> 32 us
  Pallas kernels: 0 us -> 27.7 us
  matrix products: 24 us -> 3.61 us
  starting transfers between devices: 14.2 us -> 33.8 us
  between operations: 14.2 us -> 0.82 us
  local copies, waits for them, and re-layouts: 16.3 us -> 7.56 us
    all_to_all x1, blocking collectives: 60.8 us -> 32 us  [per_device(): lax.all_to_all(outgoing, PLANE, split_axis=0, concat_axis=0, tiled=True)]
    ppermute x0 -> x17, starting transfers between devices: none -> 28.2 us  [the longest x14 27.7 us: from_line(): lax.ppermute(rows, 'z', [((i + distance) % planes, i) for i in range(plan...]
    pallas_call x0 -> x6, Pallas kernels: none -> 27.7 us  [the longest x1 15.3 us: experts(): pl.pallas_call(expert_kernel, out_shape=shape(count, width), in_specs=[pl...]
    dot_general x7 -> x3, matrix products: 24 us -> 3.61 us  [the longest x1 1.82 us: attention(): jnp.einsum('rhp,rpl->rhl', probabilities, cache_latent, preferred_element...]
    reduce_scatter x1 -> x0, waiting for transfers between devices: 18.3 us -> none  [per_device(): lax.psum_scatter(rounded.astype(jnp.bfloat16), 'cores', scatter_dimension...]
    all_to_all x1, waiting for transfers between devices: 41.7 us -> 24.2 us  [per_device(): lax.all_to_all(result, PLANE, split_axis=0, concat_axis=0, tiled=True)]
    reshape x4 -> x0, local copies, waits for them, and re-layouts: 15.2 us -> none  [the longest x1 4.92 us: per_device(): arrived = arrived.reshape(slot_count, model_width)]
    all_gather x1 -> x0, waiting for transfers between devices: 14.8 us -> none  [per_device(): both_cores = lax.all_gather(arrived, 'cores', axis=0, tiled=True)]
  transfers between devices with their start and end apart: 3 -> 18, of which waited for: 3 -> 8; matrix products, arithmetic and copies ran while one was open for 2% -> 3% of each run, Pallas kernels for 0% -> 1%
where the time goes in v1:
time: 147 us; the launch traced here: 145 us
  waiting for transfers between devices  37.1 us (25%)
  starting transfers between devices  33.8 us (23%)
  blocking collectives  32 us (22%)
  Pallas kernels  27.7 us (19%)
  local copies, waits for them, and re-layouts  7.56 us (5%)
  matrix products  3.61 us (2%)
  other arithmetic  2.95 us (2%)
    all_to_all x1, blocking collectives, per_device(): lax.all_to_all(outgoing, PLANE, split_axis=0, concat_axis=0, tiled=True)  32 us
    ppermute x14, starting transfers between devices, from_line(): lax.ppermute(rows, 'z', [((i + distance) % planes, i) for i in range(plan...  27.7 us
    all_to_all x1, waiting for transfers between devices, per_device(): lax.all_to_all(result, PLANE, split_axis=0, concat_axis=0, tiled=True)  24.2 us
    pallas_call x1, Pallas kernels, experts(): pl.pallas_call(expert_kernel, out_shape=shape(count, width), in_specs=[pl...  15.3 us
    ppermute x14, waiting for transfers between devices, from_line(): lax.ppermute(rows, 'z', [((i + distance) % planes, i) for i in range(plan...  12.8 us
    pallas_call x5, Pallas kernels, call(): pl.pallas_call(kernel, out_shape=out_shape, scratch_shapes=scratch, compi...  12.3 us
    unnamed x41, local copies, waits for them, and re-layouts  6.06 us
    all_to_all x1, starting transfers between devices, per_device(): lax.all_to_all(result, PLANE, split_axis=0, concat_axis=0, tiled=True)  5.59 us
  transfers between devices with their start and end apart: 18, of which 8 were waited for; matrix products, arithmetic and copies ran while one was open for 3% of the time, Pallas kernels for 1%

profile of v1, /device:TPU:6, one launch (start us, length us, event | category | flops | bytes accessed | tf_op | source)
XLA Modules:
  0.0 145.5 jit_solution(11129684786544384567)
XLA Ops:
  5.1 1.7 %shard_map.131.refs_0_ = bf16[16,3712]{1,0:T(8,128)(2,1)} custom-call(bf16[16,3584]{1,0:T(8,128)(2,1)} %tokens.3, f32[1,3584]{1,0:T(1,128)} %broadcast_in_dim.14.gain, bf16[16,128]{1,0:T(8,128)(2,1)} %fusion.13.tail), custom_call_target="tpu_custom_call" | custom-call | bytes 251904 | tf_op jit(solution)/shard_map/pallas_call | solution.py:40
  6.8 6.3 %collective-permute-start.1 = (bf16[16,3712]{1,0:T(8,128)(2,1)}, bf16[16,3712]{1,0:T(8,128)(2,1)S(1)}, u32[]{:S(2)}, u32[]{:S(2)}) collective-permute-start(bf16[16,3712]{1,0:T(8,128)(2,1)} %shard_map.131.refs_0_), channel_id=1, source_target_pairs={{4,0},{6,2},{8,4},{10,6},{12,8},{14,10},{0,12},{2,14},{5,1},{7,3},... | collective-permute-start | bytes 356360 | tf_op jit(solution)/shard_map/ppermute | solution.py:197
  13.1 3.7 %collective-permute-start = (bf16[16,3712]{1,0:T(8,128)(2,1)}, bf16[16,3712]{1,0:T(8,128)(2,1)S(1)}, u32[]{:S(2)}, u32[]{:S(2)}) collective-permute-start(bf16[16,3712]{1,0:T(8,128)(2,1)} %shard_map.131.refs_0_), channel_id=1, source_target_pairs={{2,0},{4,2},{6,4},{8,6},{10,8},{12,10},{14,12},{0,14},{3,1},{5,3},... | collective-permute-start | bytes 356360 | tf_op jit(solution)/shard_map/ppermute | solution.py:197
  16.7 2.5 %collective-permute-done.1.refs_2_ = bf16[16,3712]{1,0:T(8,128)(2,1)S(1)} collective-permute-done((bf16[16,3712]{1,0:T(8,128)(2,1)}, bf16[16,3712]{1,0:T(8,128)(2,1)S(1)}, u32[]{:S(2)}, u32[]{:S(2)}) %collective-permute-start.1) | collective-permute-done | bytes 118816 | tf_op jit(solution)/shard_map/ppermute | solution.py:197
  19.2 2.1 %collective-permute-start.2 = (bf16[16,3712]{1,0:T(8,128)(2,1)S(1)}, bf16[16,3712]{1,0:T(8,128)(2,1)S(1)}, u32[]{:S(2)}, u32[]{:S(2)}) collective-permute-start(bf16[16,3712]{1,0:T(8,128)(2,1)S(1)} %collective-permute-done.1.refs_2_), channel_id=1, source_target_pairs={{2,0},{4,2},{6,4},{8,6},{10,8},{12,10},{14,12},{0,14},{3,1},{5,3},... | collective-permute-start | bytes 356360 | tf_op jit(solution)/shard_map/ppermute | solution.py:197
  21.3 2.4 %collective-permute-start.3 = (bf16[16,3712]{1,0:T(8,128)(2,1)S(1)}, bf16[16,3712]{1,0:T(8,128)(2,1)S(1)}, u32[]{:S(2)}, u32[]{:S(2)}) collective-permute-start(bf16[16,3712]{1,0:T(8,128)(2,1)S(1)} %collective-permute-done.1.refs_2_), channel_id=1, source_target_pairs={{4,0},{6,2},{8,4},{10,6},{12,8},{14,10},{0,12},{2,14},{5,1},{7,3},... | collective-permute-start | bytes 356360 | tf_op jit(solution)/shard_map/ppermute | solution.py:197
  23.7 2.0 %collective-permute-start.5 = (bf16[16,3712]{1,0:T(8,128)(2,1)S(1)}, bf16[16,3712]{1,0:T(8,128)(2,1)S(1)}, u32[]{:S(2)}, u32[]{:S(2)}) collective-permute-start(bf16[16,3712]{1,0:T(8,128)(2,1)S(1)} %collective-permute-done.4.refs_6_), channel_id=1, source_target_pairs={{14,0},{0,2},{2,4},{4,6},{6,8},{8,10},{10,12},{12,14},{15,1},{1,3}... | collective-permute-start | bytes 356360 | tf_op jit(solution)/shard_map/ppermute | solution.py:197
  26.4 2.5 %collective-permute-done.3.refs_4_ = bf16[16,3712]{1,0:T(8,128)(2,1)S(1)} collective-permute-done((bf16[16,3712]{1,0:T(8,128)(2,1)S(1)}, bf16[16,3712]{1,0:T(8,128)(2,1)S(1)}, u32[]{:S(2)}, u32[]{:S(2)}) %collective-permute-start.3) | collective-permute-done | bytes 118816 | tf_op jit(solution)/shard_map/ppermute | solution.py:197
  30.5 3.7 %shard_map.132 = (bf16[256,3584]{1,0:T(8,128)(2,1)}, f32[128,256]{1,0:T(8,128)}) custom-call(f32[1,256]{1,0:T(1,128)} %fusion.16.own, bf16[16,3712]{1,0:T(8,128)(2,1)} %shard_map.131.refs_0_, bf16[16,3712]{1,0:T(8,128)(2,1)} %copy-done.6, bf16[16,3712]{1,0:T(8,128)(2,1)} %copy-done.4, bf16[16,3712]{1,0:T(8,128)(2,1)} %copy-done.8, ...), custom_call_target="tpu_custom_call" | custom-call | bytes 2917376 | tf_op jit(solution)/shard_map/pallas_call | solution.py:40
  34.7 32.0 %all_to_all.22 = bf16[16,16,3584]{2,1,0:T(8,128)(2,1)} all-to-all(bf16[16,16,3584]{2,1,0:T(8,128)(2,1)} %bitcast.23), channel_id=1, replica_groups=mesh['xl'=2,'y'=4,'xh'=2,'z'=8,'c'=2] {'xl','y','xh'}, dimensions={0} | all-to-all | bytes 3670016 | tf_op jit(solution)/shard_map/all_to_all | solution.py:252
  66.7 1.9 %copy-done.2 = bf16[3584,512]{1,0:T(8,128)(2,1)} copy-done((bf16[3584,512]{1,0:T(8,128)(2,1)}, bf16[3584,512]{1,0:T(8,128)(2,1)S(1)}, u32[]{:S(2)}) %copy-start.2) | copy-done | bytes 3670040
  68.6 15.3 %shard_map.133 = bf16[256,3584]{1,0:T(8,128)(2,1)} custom-call(bf16[256,3584]{1,0:T(8,128)(2,1)} %bitcast.14, bf16[3584,512]{1,0:T(8,128)(2,1)} %bitcast.18, bf16[3584,512]{1,0:T(8,128)(2,1)} %bitcast.20, bf16[512,3584]{1,0:T(8,128)(2,1)} %bitcast.22, bf16[3584,512]{1,0:T(8,128)(2,1)} %copy-done.2, bf16[3584,512]{1,0:T(8,128)(2,1)} %collective-permute-done.8.refs_4_, ...), custom_call_target="tpu_custom_call" | custom-call | flops 5637144576 | bytes 22020096 | tf_op jit(solution)/shard_map/pallas_call | solution.py:181
  84.0 5.6 %all-to-all-start.1 = ((bf16[16,16,3584]{2,1,0:T(8,128)(2,1)}), bf16[16,16,3584]{2,1,0:T(8,128)(2,1)S(1)}, u32[]{:S(2)}, u32[]{:S(2)}) async-start(bf16[16,16,3584]{2,1,0:T(8,128)(2,1)} %bitcast.15), calls=%async_computation.1 | async-start | bytes 3670016 | tf_op jit(solution)/shard_map/all_to_all | solution.py:254
  89.9 1.5 %fusion.3 = f32[4,128,256]{2,1,0:T(8,128)S(1)} fusion(f32[4,128,256]{2,1,0:T(8,128)S(1)} %fusion.19, bf16[4,128,512]{2,1,0:T(8,128)(2,1)} %param.19, bf16[4,256,512]{2,1,0:T(8,128)(2,1)S(1)} %copy-done, pred[4,256]{1,0:T(4,128)(4,1)S(1)} %iota_compare_fusion.1), kind=kOutput, calls=%fused_computation.5 | convolution fusion | flops 134610944 | bytes 2622464 | tf_op jit(solution)/shard_map/rhl,rpl->rhp/dot_general | solution.py:19
  91.5 24.2 %all-to-all-done.1 = bf16[16,16,3584]{2,1,0:T(8,128)(2,1)S(1)} async-done(((bf16[16,16,3584]{2,1,0:T(8,128)(2,1)}), bf16[16,16,3584]{2,1,0:T(8,128)(2,1)S(1)}, u32[]{:S(2)}, u32[]{:S(2)}) %all-to-all-start.1) | async-done | bytes 1835040 | tf_op jit(solution)/shard_map/all_to_all | solution.py:254
  117.0 3.1 %shard_map.134 = (f32[16,3584]{1,0:T(8,128)}, bf16[16,3584]{1,0:T(8,128)(2,1)}, bf16[16,3584]{1,0:T(8,128)(2,1)}, bf16[16,3584]{1,0:T(8,128)(2,1)}, bf16[16,3584...) custom-call(f32[128,256]{1,0:T(8,128)} %get-tuple-element.18.scale, ...), custom_call_target="tpu_custom_call" | custom-call | bytes 2998272 | tf_op jit(solution)/shard_map/pallas_call | solution.py:40
  121.0 2.3 %collective-permute-start.13 = (bf16[16,3584]{1,0:T(8,128)(2,1)}, bf16[16,3584]{1,0:T(8,128)(2,1)S(1)}, u32[]{:S(2)}, u32[]{:S(2)}) collective-permute-start(bf16[16,3584]{1,0:T(8,128)(2,1)} %get-tuple-element.29), channel_id=1, source_target_pairs={{12,0},{14,2},{0,4},{2,6},{4,8},{6,10},{8,12},{10,14},{13,1},{15,3... | collective-permute-start | bytes 344072 | tf_op jit(solution)/shard_map/ppermute | solution.py:197
  124.1 1.6 %collective-permute-start.10 = (bf16[16,3584]{1,0:T(8,128)(2,1)}, bf16[16,3584]{1,0:T(8,128)(2,1)S(1)}, u32[]{:S(2)}, u32[]{:S(2)}) collective-permute-start(bf16[16,3584]{1,0:T(8,128)(2,1)} %get-tuple-element.25), channel_id=1, source_target_pairs={{14,0},{0,2},{2,4},{4,6},{6,8},{8,10},{10,12},{12,14},{15,1},{1,3}... | collective-permute-start | bytes 344072 | tf_op jit(solution)/shard_map/ppermute | solution.py:197
  125.7 1.7 %collective-permute-start.11 = (bf16[16,3584]{1,0:T(8,128)(2,1)}, bf16[16,3584]{1,0:T(8,128)(2,1)S(1)}, u32[]{:S(2)}, u32[]{:S(2)}) collective-permute-start(bf16[16,3584]{1,0:T(8,128)(2,1)} %get-tuple-element.26), channel_id=1, source_target_pairs={{2,0},{4,2},{6,4},{8,6},{10,8},{12,10},{14,12},{0,14},{3,1},{5,3},... | collective-permute-start | bytes 344072 | tf_op jit(solution)/shard_map/ppermute | solution.py:197
  128.8 3.0 %collective-permute-done.13.across = bf16[16,3584]{1,0:T(8,128)(2,1)S(1)} collective-permute-done((bf16[16,3584]{1,0:T(8,128)(2,1)}, bf16[16,3584]{1,0:T(8,128)(2,1)S(1)}, u32[]{:S(2)}, u32[]{:S(2)}) %collective-permute-start.13) | collective-permute-done | bytes 114720 | tf_op jit(solution)/shard_map/ppermute | solution.py:197
  132.6 1.8 %shard_map.135 = (bf16[16,3584]{1,0:T(8,128)(2,1)}, bf16[16,3584]{1,0:T(8,128)(2,1)}) custom-call(bf16[16,3584]{1,0:T(8,128)(2,1)} %get-tuple-element.27.up2, bf16[16,3584]{1,0:T(8,128)(2,1)} %copy-done.15, bf16[16,3584]{1,0:T(8,128)(2,1)} %copy-done.16, bf16[16,3584]{1,0:T(8,128)(2,1)} %get-tuple-element.30.down2, bf16[16,3584]{1,0:T(8,128)(2,1)} %copy-done.17), custom_call_target="tpu_custom_call" | custom-call | bytes 802816 | tf_op jit(solution)/shard_map/pallas_call | solution.py:40
  135.5 3.1 %collective-permute-start.16 = (bf16[16,3584]{1,0:T(8,128)(2,1)}, bf16[16,3584]{1,0:T(8,128)(2,1)S(1)}, u32[]{:S(2)}, u32[]{:S(2)}) collective-permute-start(bf16[16,3584]{1,0:T(8,128)(2,1)} %get-tuple-element.33), channel_id=1, source_target_pairs={{4,0},{6,2},{8,4},{10,6},{12,8},{14,10},{0,12},{2,14},{5,1},{7,3},... | collective-permute-start | bytes 344072 | tf_op jit(solution)/shard_map/ppermute | solution.py:197
  138.5 1.8 %convolution_convert_fusion = bf16[4,128,512]{2,1,0:T(8,128)(2,1)} fusion(bf16[4,256,512]{2,1,0:T(8,128)(2,1)S(1)} %copy-done, f32[4,128]{1,0:T(4,128)S(1)} %fusion.18, f32[4,128,256]{2,1,0:T(8,128)S(1)} %fusion.3), kind=kOutput, calls=%fused_computation.1 | convolution fusion | flops 134873856 | bytes 2099200 | tf_op jit(solution)/shard_map/rhp,rpl->rhl/dot_general | solution.py:31
  143.6 1.9 %shard_map.136 = bf16[16,3584]{1,0:T(8,128)(2,1)} custom-call(bf16[16,3584]{1,0:T(8,128)(2,1)} %tokens.3, f32[16,3584]{1,0:T(8,128)} %get-tuple-element.24.own, bf16[16,3584]{1,0:T(8,128)(2,1)} %copy-done.11, bf16[16,3584]{1,0:T(8,128)(2,1)} %copy-done.12, bf16[16,3584]{1,0:T(8,128)(2,1)} %copy-done.13, bf16[16,3584]{1,0:T(8,128)(2,1)} %copy-done.14), custom_call_target="tpu_custom_call" | custom-call | bytes 917504 | tf_op jit(solution)/shard_map/pallas_call | solution.py:40
  (73 shorter events, 16.7 us)
Async XLA Ops:
  0.6 89.3 %copy-start = (bf16[4,256,512]{2,1,0:T(8,128)(2,1)S(1)}, bf16[4,256,512]{2,1,0:T(8,128)(2,1)}, u32[]{:S(2)}) copy-start(bf16[4,256,512]{2,1,0:T(8,128)(2,1)} %param.21) | copy-start | bytes 3145732
  6.8 12.5 %collective-permute-start.1 = (bf16[16,3712]{1,0:T(8,128)(2,1)}, bf16[16,3712]{1,0:T(8,128)(2,1)S(1)}, u32[]{:S(2)}, u32[]{:S(2)}) collective-permute-start(bf16[16,3712]{1,0:T(8,128)(2,1)} %shard_map.131.refs_0_), channel_id=1, source_target_pairs={{4,0},{6,2},{8,4},{10,6},{12,8},{14,10},{0,12},{2,14},{5,1},{7,3},... | collective-permute-start | bytes 356360 | tf_op jit(solution)/shard_map/ppermute | solution.py:197
  13.1 10.7 %collective-permute-start.4 = (bf16[16,3712]{1,0:T(8,128)(2,1)}, bf16[16,3712]{1,0:T(8,128)(2,1)S(1)}, u32[]{:S(2)}, u32[]{:S(2)}) collective-permute-start(bf16[16,3712]{1,0:T(8,128)(2,1)} %shard_map.131.refs_0_), channel_id=1, source_target_pairs={{12,0},{14,2},{0,4},{2,6},{4,8},{6,10},{8,12},{10,14},{13,1},{15,3... | collective-permute-start | bytes 356360 | tf_op jit(solution)/shard_map/ppermute | solution.py:197
  13.1 13.3 %collective-permute-start = (bf16[16,3712]{1,0:T(8,128)(2,1)}, bf16[16,3712]{1,0:T(8,128)(2,1)S(1)}, u32[]{:S(2)}, u32[]{:S(2)}) collective-permute-start(bf16[16,3712]{1,0:T(8,128)(2,1)} %shard_map.131.refs_0_), channel_id=1, source_target_pairs={{2,0},{4,2},{6,4},{8,6},{10,8},{12,10},{14,12},{0,14},{3,1},{5,3},... | collective-permute-start | bytes 356360 | tf_op jit(solution)/shard_map/ppermute | solution.py:197
  16.7 9.6 %collective-permute-start.6 = (bf16[16,3712]{1,0:T(8,128)(2,1)}, bf16[16,3712]{1,0:T(8,128)(2,1)S(1)}, u32[]{:S(2)}, u32[]{:S(2)}) collective-permute-start(bf16[16,3712]{1,0:T(8,128)(2,1)} %shard_map.131.refs_0_), channel_id=1, source_target_pairs={{14,0},{0,2},{2,4},{4,6},{6,8},{8,10},{10,12},{12,14},{15,1},{1,3}... | collective-permute-start | bytes 356360 | tf_op jit(solution)/shard_map/ppermute | solution.py:197
  19.2 10.5 %copy-start.4 = (bf16[16,3712]{1,0:T(8,128)(2,1)}, bf16[16,3712]{1,0:T(8,128)(2,1)S(1)}, u32[]{:S(2)}) copy-start(bf16[16,3712]{1,0:T(8,128)(2,1)S(1)} %collective-permute-done.1.refs_2_) | copy-start | bytes 356356
  19.2 7.1 %collective-permute-start.2 = (bf16[16,3712]{1,0:T(8,128)(2,1)S(1)}, bf16[16,3712]{1,0:T(8,128)(2,1)S(1)}, u32[]{:S(2)}, u32[]{:S(2)}) collective-permute-start(bf16[16,3712]{1,0:T(8,128)(2,1)S(1)} %collective-permute-done.1.refs_2_), channel_id=1, source_target_pairs={{2,0},{4,2},{6,4},{8,6},{10,8},{12,10},{14,12},{0,14},{3,1},{5,3},... | collective-permute-start | bytes 356360 | tf_op jit(solution)/shard_map/ppermute | solution.py:197
  21.3 7.5 %collective-permute-start.3 = (bf16[16,3712]{1,0:T(8,128)(2,1)S(1)}, bf16[16,3712]{1,0:T(8,128)(2,1)S(1)}, u32[]{:S(2)}, u32[]{:S(2)}) collective-permute-start(bf16[16,3712]{1,0:T(8,128)(2,1)S(1)} %collective-permute-done.1.refs_2_), channel_id=1, source_target_pairs={{4,0},{6,2},{8,4},{10,6},{12,8},{14,10},{0,12},{2,14},{5,1},{7,3},... | collective-permute-start | bytes 356360 | tf_op jit(solution)/shard_map/ppermute | solution.py:197
  23.7 6.1 %copy-start.5 = (bf16[16,3712]{1,0:T(8,128)(2,1)}, bf16[16,3712]{1,0:T(8,128)(2,1)S(1)}, u32[]{:S(2)}) copy-start(bf16[16,3712]{1,0:T(8,128)(2,1)S(1)} %collective-permute-done.4.refs_6_) | copy-start | bytes 356356
  23.7 6.0 %collective-permute-start.5 = (bf16[16,3712]{1,0:T(8,128)(2,1)S(1)}, bf16[16,3712]{1,0:T(8,128)(2,1)S(1)}, u32[]{:S(2)}, u32[]{:S(2)}) collective-permute-start(bf16[16,3712]{1,0:T(8,128)(2,1)S(1)} %collective-permute-done.4.refs_6_), channel_id=1, source_target_pairs={{14,0},{0,2},{2,4},{4,6},{6,8},{8,10},{10,12},{12,14},{15,1},{1,3}... | collective-permute-start | bytes 356360 | tf_op jit(solution)/shard_map/ppermute | solution.py:197
  34.2 32.5 %collective-permute-start.7 = (bf16[3584,512]{1,0:T(8,128)(2,1)}, bf16[3584,512]{1,0:T(8,128)(2,1)S(1)}, u32[]{:S(2)}, u32[]{:S(2)}) collective-permute-start(bf16[3584,512]{1,0:T(8,128)(2,1)} %bitcast.17), channel_id=1, source_target_pairs={{0,1},{1,0},{2,3},{3,2},{4,5},{5,4},{6,7},{7,6},{8,9},{9,8},{10,11... | collective-permute-start | bytes 11010056 | tf_op jit(solution)/shard_map/ppermute | solution.py:251
  34.2 32.5 %collective-permute-start.8 = (bf16[3584,512]{1,0:T(8,128)(2,1)}, bf16[3584,512]{1,0:T(8,128)(2,1)}, u32[]{:S(2)}, u32[]{:S(2)}) collective-permute-start(bf16[3584,512]{1,0:T(8,128)(2,1)} %bitcast.19), channel_id=1, source_target_pairs={{0,1},{1,0},{2,3},{3,2},{4,5},{5,4},{6,7},{7,6},{8,9},{9,8},{10,11... | collective-permute-start | bytes 11010056 | tf_op jit(solution)/shard_map/ppermute | solution.py:251
  34.7 32.0 %collective-permute-start.9 = (bf16[512,3584]{1,0:T(8,128)(2,1)}, bf16[512,3584]{1,0:T(8,128)(2,1)}, u32[]{:S(2)}, u32[]{:S(2)}) collective-permute-start(bf16[512,3584]{1,0:T(8,128)(2,1)} %bitcast.21), channel_id=1, source_target_pairs={{0,1},{1,0},{2,3},{3,2},{4,5},{5,4},{6,7},{7,6},{8,9},{9,8},{10,11... | collective-permute-start | bytes 11010056 | tf_op jit(solution)/shard_map/ppermute | solution.py:251
  83.9 5.6 %copy-start.19 = (s32[4]{0:T(128)S(1)}, s32[4]{0:T(128)}, u32[]{:S(2)}) copy-start(s32[4]{0:T(128)} %param.23) | copy-start | bytes 52
  84.0 5.7 %copy-start.3 = (bf16[4,64,256]{2,1,0:T(8,128)(2,1)S(1)}, bf16[4,64,256]{2,1,0:T(8,128)(2,1)}, u32[]{:S(2)}) copy-start(bf16[4,64,256]{2,1,0:T(8,128)(2,1)} %param.22) | copy-start | bytes 393220
  84.0 5.7 %copy-start.18 = (bf16[4,128,64]{1,2,0:T(8,128)(2,1)S(1)}, bf16[4,128,64]{1,2,0:T(8,128)(2,1)}, u32[]{:S(2)}) copy-start(bf16[4,128,64]{1,2,0:T(8,128)(2,1)} %param.20) | copy-start | bytes 196612
  84.0 31.7 %all-to-all-start.1 = ((bf16[16,16,3584]{2,1,0:T(8,128)(2,1)}), bf16[16,16,3584]{2,1,0:T(8,128)(2,1)S(1)}, u32[]{:S(2)}, u32[]{:S(2)}) async-start(bf16[16,16,3584]{2,1,0:T(8,128)(2,1)} %bitcast.15), calls=%async_computation.1 | async-start | bytes 3670016 | tf_op jit(solution)/shard_map/all_to_all | solution.py:254
  120.1 8.7 %collective-permute-start.12 = (bf16[16,3584]{1,0:T(8,128)(2,1)}, bf16[16,3584]{1,0:T(8,128)(2,1)S(1)}, u32[]{:S(2)}, u32[]{:S(2)}) collective-permute-start(bf16[16,3584]{1,0:T(8,128)(2,1)} %get-tuple-element.28), channel_id=1, source_target_pairs={{14,0},{0,2},{2,4},{4,6},{6,8},{8,10},{10,12},{12,14},{15,1},{1,3}... | collective-permute-start | bytes 344072 | tf_op jit(solution)/shard_map/ppermute | solution.py:197
  121.0 10.9 %collective-permute-start.13 = (bf16[16,3584]{1,0:T(8,128)(2,1)}, bf16[16,3584]{1,0:T(8,128)(2,1)S(1)}, u32[]{:S(2)}, u32[]{:S(2)}) collective-permute-start(bf16[16,3584]{1,0:T(8,128)(2,1)} %get-tuple-element.29), channel_id=1, source_target_pairs={{12,0},{14,2},{0,4},{2,6},{4,8},{6,10},{8,12},{10,14},{13,1},{15,3... | collective-permute-start | bytes 344072 | tf_op jit(solution)/shard_map/ppermute | solution.py:197
  123.3 8.5 %collective-permute-start.14 = (bf16[16,3584]{1,0:T(8,128)(2,1)}, bf16[16,3584]{1,0:T(8,128)(2,1)S(1)}, u32[]{:S(2)}, u32[]{:S(2)}) collective-permute-start(bf16[16,3584]{1,0:T(8,128)(2,1)} %get-tuple-element.31), channel_id=1, source_target_pairs={{2,0},{4,2},{6,4},{8,6},{10,8},{12,10},{14,12},{0,14},{3,1},{5,3},... | collective-permute-start | bytes 344072 | tf_op jit(solution)/shard_map/ppermute | solution.py:197
  124.1 16.2 %collective-permute-start.10 = (bf16[16,3584]{1,0:T(8,128)(2,1)}, bf16[16,3584]{1,0:T(8,128)(2,1)S(1)}, u32[]{:S(2)}, u32[]{:S(2)}) collective-permute-start(bf16[16,3584]{1,0:T(8,128)(2,1)} %get-tuple-element.25), channel_id=1, source_target_pairs={{14,0},{0,2},{2,4},{4,6},{6,8},{8,10},{10,12},{12,14},{15,1},{1,3}... | collective-permute-start | bytes 344072 | tf_op jit(solution)/shard_map/ppermute | solution.py:197
  125.7 14.7 %collective-permute-start.11 = (bf16[16,3584]{1,0:T(8,128)(2,1)}, bf16[16,3584]{1,0:T(8,128)(2,1)S(1)}, u32[]{:S(2)}, u32[]{:S(2)}) collective-permute-start(bf16[16,3584]{1,0:T(8,128)(2,1)} %get-tuple-element.26), channel_id=1, source_target_pairs={{2,0},{4,2},{6,4},{8,6},{10,8},{12,10},{14,12},{0,14},{3,1},{5,3},... | collective-permute-start | bytes 344072 | tf_op jit(solution)/shard_map/ppermute | solution.py:197
  134.4 7.2 %collective-permute-start.15 = (bf16[16,3584]{1,0:T(8,128)(2,1)}, bf16[16,3584]{1,0:T(8,128)(2,1)S(1)}, u32[]{:S(2)}, u32[]{:S(2)}) collective-permute-start(bf16[16,3584]{1,0:T(8,128)(2,1)} %get-tuple-element.32), channel_id=1, source_target_pairs={{12,0},{14,2},{0,4},{2,6},{4,8},{6,10},{8,12},{10,14},{13,1},{15,3... | collective-permute-start | bytes 344072 | tf_op jit(solution)/shard_map/ppermute | solution.py:197
  135.5 7.5 %collective-permute-start.16 = (bf16[16,3584]{1,0:T(8,128)(2,1)}, bf16[16,3584]{1,0:T(8,128)(2,1)S(1)}, u32[]{:S(2)}, u32[]{:S(2)}) collective-permute-start(bf16[16,3584]{1,0:T(8,128)(2,1)} %get-tuple-element.33), channel_id=1, source_target_pairs={{4,0},{6,2},{8,4},{10,6},{12,8},{14,10},{0,12},{2,14},{5,1},{7,3},... | collective-permute-start | bytes 344072 | tf_op jit(solution)/shard_map/ppermute | solution.py:197
  (14 other events, 26.5 us)

commit v2 on v1

v2 whole, which is shorter than its diff:
```python
import functools
import jax
import jax.numpy as jnp
from jax import lax
from jax.experimental import pallas as pl
from jax.experimental.pallas import tpu as pltpu
from jax.sharding import Mesh, PartitionSpec as P

score_scale = 192.0 ** (-0.5)
epsilon = 1e-06
PLANE = ("xl", "y", "xh")
EXPERT = ("xl", "y", "xh", "z")
ALL = ("xl", "y", "xh", "z", "c")
TAIL = 128
STEP = 512
MIB = 1024 * 1024


def attention(query_latent, query_rope, cache_latent, cache_rope, lengths):
    scores = jnp.einsum(
        "rhl,rpl->rhp", query_latent, cache_latent, preferred_element_type=jnp.float32
    )
    scores = (
        scores
        + jnp.einsum("rhk,rkp->rhp", query_rope, cache_rope, preferred_element_type=jnp.float32)
    ) * score_scale
    in_range = jnp.arange(cache_latent.shape[1], dtype=jnp.int32)[None, :] < lengths[:, None]
    scores = jnp.where(in_range[:, None, :], scores, -1e30)
    highest = jnp.max(scores, axis=2, keepdims=True)
    weights = jnp.exp(scores - highest)
    probabilities = (weights / jnp.sum(weights, axis=2, keepdims=True)).astype(jnp.bfloat16)
    return jnp.einsum(
        "rhp,rpl->rhl", probabilities, cache_latent, preferred_element_type=jnp.float32
    ).astype(jnp.bfloat16)


def call(kernel, out_shape, *operands, limit, flops=0, scratch=()):
    moved = sum(x.size * x.dtype.itemsize for x in operands) + sum(
        x.size * x.dtype.itemsize for x in jax.tree.leaves(out_shape)
    )
    return pl.pallas_call(
        kernel,
        out_shape=out_shape,
        scratch_shapes=scratch,
        compiler_params=pltpu.CompilerParams(vmem_limit_bytes=limit * MIB),
        cost_estimate=pl.CostEstimate(flops=flops, bytes_accessed=moved, transcendentals=0),
    )(*operands)


def shape(*dims, dtype=jnp.bfloat16):
    return jax.ShapeDtypeStruct(dims, dtype)


def in_hbm(x):
    return pltpu.with_memory_space_constraint(x, pltpu.HBM)


def norm_kernel(tokens_in, gain_in, routes_in, weight_in, packed, tokens, gain, routes, route_weight, sems):
    copies = [
        pltpu.make_async_copy(source, target, sems.at[i])
        for i, (source, target) in enumerate(
            (
                (routes_in, routes),
                (weight_in, route_weight),
                (tokens_in, tokens),
                (gain_in, gain.at[0]),
            )
        )
    ]
    for copy in copies:
        copy.start()
    width = tokens.shape[1]
    top = routes.shape[0]
    copies[0].wait()
    copies[1].wait()
    weight = route_weight[...]
    high = weight.astype(jnp.bfloat16).astype(jnp.float32)
    middle = (weight - high).astype(jnp.bfloat16).astype(jnp.float32)
    low = weight - high - middle
    columns = jnp.concatenate([routes[...].astype(jnp.float32), high, middle, low], axis=0)
    row = lax.broadcasted_iota(jnp.int32, (4 * top, TAIL), 0)
    column = lax.broadcasted_iota(jnp.int32, (4 * top, TAIL), 1)
    unit = jnp.where(row == column, 1.0, 0.0).astype(jnp.bfloat16)
    packed[:, width:] = lax.dot_general(
        columns.astype(jnp.bfloat16),
        unit,
        (((0,), (0,)), ((), ())),
        preferred_element_type=jnp.float32,
    ).astype(jnp.bfloat16)
    copies[2].wait()
    widened = tokens[...].astype(jnp.float32)
    inverse = lax.rsqrt(jnp.mean(widened * widened, axis=1, keepdims=True) + epsilon)
    copies[3].wait()
    packed[:, :width] = (widened * inverse * gain[...]).astype(jnp.bfloat16)


def normalize(tokens, gain, routes, route_weight):
    operands = (tokens, gain, routes.T, route_weight.T)
    return pl.pallas_call(
        norm_kernel,
        out_shape=shape(tokens.shape[0], tokens.shape[1] + TAIL),
        in_specs=[pl.BlockSpec(memory_space=pltpu.HBM)] * 4,
        scratch_shapes=[
            pltpu.VMEM(tokens.shape, tokens.dtype),
            pltpu.VMEM((1,) + gain.shape, gain.dtype),
            pltpu.VMEM(operands[2].shape, routes.dtype),
            pltpu.VMEM(operands[3].shape, route_weight.dtype),
            pltpu.SemaphoreType.DMA((4,)),
        ],
        compiler_params=pltpu.CompilerParams(vmem_limit_bytes=4 * MIB),
        cost_estimate=pl.CostEstimate(
            flops=4 * tokens.size, bytes_accessed=4 * tokens.size, transcendentals=0
        ),
    )(*(in_hbm(x) for x in operands))


def slots_of(info, experts, count, top):
    gathered, places = info.shape[0], experts.shape[1]
    names = jnp.zeros((gathered, places), jnp.float32)
    weight = jnp.zeros((gathered, places), jnp.float32)
    for k in range(top):
        match = info[:, k : k + 1] == experts
        share = (
            info[:, top + k : top + k + 1]
            + info[:, 2 * top + k : 2 * top + k + 1]
            + info[:, 3 * top + k : 3 * top + k + 1]
        )
        names = jnp.where(match, 1.0, names)
        weight = weight + jnp.where(match, share, 0.0)
    row = lax.broadcasted_iota(jnp.int32, (gathered, gathered), 0)
    column = lax.broadcasted_iota(jnp.int32, (gathered, gathered), 1)
    before = jnp.where((column < row) & (column // count == row // count), 1.0, 0.0)
    rank = jnp.dot(
        before.astype(jnp.bfloat16), names.astype(jnp.bfloat16), preferred_element_type=jnp.float32
    )
    token = lax.broadcasted_iota(jnp.int32, (gathered, places), 0)
    slot = lax.broadcasted_iota(jnp.int32, (gathered, places), 1) % (2 * gathered // count)
    here = (names > 0.0) & ((token // count) * 2 + rank.astype(jnp.int32) == slot)
    return jnp.where(here, 1.0, 0.0), jnp.where(here, weight, 0.0)


def dispatch_kernel(top, own, own_half, *refs):
    blocks, (outgoing, near_scale, far_scale, built, sems) = refs[:-5], refs[-5:]
    count = blocks[0].shape[0]
    half = count * len(blocks) // 2
    width = outgoing.shape[1]
    info = jnp.concatenate([b[:, width:] for b in blocks], axis=0).astype(jnp.float32)
    place, _ = slots_of(info, own[...], count, top)
    place = place.astype(jnp.bfloat16)
    copies = []
    for i, start in enumerate(range(0, width, STEP)):
        cut = pl.ds(start, STEP)
        rows = jnp.concatenate([b[:, start : start + STEP] for b in blocks], axis=0)
        built[:, cut] = lax.dot_general(
            place, rows, (((0,), (0,)), ((), ())), preferred_element_type=jnp.float32
        ).astype(jnp.bfloat16)
        copies.append(pltpu.make_async_copy(built.at[:, cut], outgoing.at[:, cut], sems.at[i]))
        copies[-1].start()
    _, near_scale[...] = slots_of(info[:half], own_half[...], count, top)
    _, far_scale[...] = slots_of(info[half:], own_half[...], count, top)
    for copy in copies:
        copy.wait()


def dispatch(top, rows, width, own, own_half, *blocks):
    gathered = blocks[0].shape[0] * len(blocks)
    any_vmem = pl.BlockSpec(memory_space=pltpu.VMEM)
    return pl.pallas_call(
        functools.partial(dispatch_kernel, top),
        out_shape=[pltpu.HBM((rows, width), jnp.bfloat16)]
        + [shape(gathered // 2, rows // 2, dtype=jnp.float32)] * 2,
        out_specs=[pl.BlockSpec(memory_space=pltpu.HBM), any_vmem, any_vmem],
        scratch_shapes=[
            pltpu.VMEM((rows, width), jnp.bfloat16),
            pltpu.SemaphoreType.DMA((width // STEP,)),
        ],
        compiler_params=pltpu.CompilerParams(vmem_limit_bytes=10 * MIB),
        cost_estimate=pl.CostEstimate(
            flops=2 * rows * gathered * width,
            bytes_accessed=4 * rows * width,
            transcendentals=0,
        ),
    )(own, own_half, *blocks)


def weighted(scale, rows):
    high = scale.astype(jnp.bfloat16)
    low = (scale - high.astype(jnp.float32)).astype(jnp.bfloat16)
    return jnp.dot(high, rows, preferred_element_type=jnp.float32) + jnp.dot(
        low, rows, preferred_element_type=jnp.float32
    )


def far_kernel(scale, returned, *blocks):
    count, width = blocks[0].shape
    step = 512
    for start in range(0, width, step):
        cut = slice(start, start + step)
        sums = weighted(scale[...], returned[:, cut])
        for i, block in enumerate(blocks):
            block[:, cut] = sums[i * count : (i + 1) * count].astype(block.dtype)


def near_kernel(scale, returned, up3, across, down3, down2_far, own, up1, down1, up2, down2):
    count, width = own.shape
    f32 = jnp.float32
    step = 512
    for start in range(0, width, step):
        cut = slice(start, start + step)
        sums = weighted(scale[...], returned[:, cut])
        own[:, cut] = sums[:count]
        up1[:, cut] = sums[count : 2 * count].astype(jnp.bfloat16)
        down1[:, cut] = sums[2 * count : 3 * count].astype(jnp.bfloat16)
        up2[:, cut] = (
            sums[3 * count :] + up3[:, cut].astype(f32) + across[:, cut].astype(f32)
        ).astype(jnp.bfloat16)
    down2[...] = (down2_far[...] + down3[...].astype(f32)).astype(jnp.bfloat16)


def final_kernel(tokens, own, *refs):
    total = own[...]
    for part in refs[:-1]:
        total = total + part[...].astype(jnp.float32)
    refs[-1][...] = (tokens[...].astype(jnp.float32) + total).astype(jnp.bfloat16)


def expert_kernel(rows, *refs):
    weights, (near, far), held = refs[:6], refs[6:8], refs[8:14]
    near_built, far_built, total, sems, out_sems = refs[14:]
    width = near.shape[1]
    copies = [pltpu.make_async_copy(weights[i], held[i], sems.at[i]) for i in range(6)]
    for copy in copies:
        copy.start()
    x = rows[...]
    sent = []
    for half in range(2):
        gate_copy, up_copy, down_copy = copies[3 * half : 3 * half + 3]
        gate_half, up_half, down_half = held[3 * half : 3 * half + 3]
        gate_copy.wait()
        gate = jnp.dot(x, gate_half[...], preferred_element_type=jnp.float32)
        up_copy.wait()
        up = jnp.dot(x, up_half[...], preferred_element_type=jnp.float32)
        activation = (gate / (1.0 + jnp.exp(-gate)) * up).astype(jnp.bfloat16)
        down_copy.wait()
        for i, start in enumerate(range(0, width, STEP)):
            cut = pl.ds(start, STEP)
            partial = jnp.dot(
                activation, down_half[:, cut], preferred_element_type=jnp.float32
            ).astype(jnp.bfloat16)
            if half == 0:
                total[:, cut] = partial
                continue
            sums = total[:, cut].astype(jnp.float32) + partial.astype(jnp.float32)
            sums = sums.reshape(-1, 2, 8, STEP)
            for j, (built, out) in enumerate(((near_built, near), (far_built, far))):
                built[:, cut] = sums[:, j].reshape(-1, STEP).astype(jnp.bfloat16)
                sent.append(
                    pltpu.make_async_copy(built.at[:, cut], out.at[:, cut], out_sems.at[j, i])
                )
                sent[-1].start()
    for copy in sent:
        copy.wait()


def experts(rows, weights):
    count, width = rows.shape
    hbm = pl.BlockSpec(memory_space=pltpu.HBM)
    half = (count // 2, width)
    return pl.pallas_call(
        expert_kernel,
        out_shape=[pltpu.HBM(half, rows.dtype)] * 2,
        in_specs=[pl.BlockSpec(memory_space=pltpu.VMEM)] + [hbm] * 6,
        out_specs=[hbm] * 2,
        scratch_shapes=[pltpu.VMEM(w.shape, w.dtype) for w in weights]
        + [pltpu.VMEM(half, rows.dtype)] * 2
        + [
            pltpu.VMEM(rows.shape, rows.dtype),
            pltpu.SemaphoreType.DMA((6,)),
            pltpu.SemaphoreType.DMA((2, width // STEP)),
        ],
        compiler_params=pltpu.CompilerParams(vmem_limit_bytes=40 * MIB),
        cost_estimate=pl.CostEstimate(
            flops=2 * count * sum(w.size for w in weights),
            bytes_accessed=2 * sum(w.size for w in weights),
            transcendentals=0,
        ),
    )(rows, *(in_hbm(w) for w in weights))


def from_line(rows, distance):
    planes = lax.axis_size("z")
    return lax.ppermute(rows, "z", [((i + distance) % planes, i) for i in range(planes)])


def per_device(
    tokens,
    norm_gain,
    routes,
    route_weight,
    w_gate,
    w_up,
    w_down,
    query_latent,
    query_rope,
    cache_latent,
    cache_rope,
    lengths,
):
    planes = lax.axis_size("z")
    places = lax.axis_size(PLANE)
    count, top = routes.shape
    width = tokens.shape[1]
    slots = 2 * planes
    rows = places * slots
    gathered = count * planes
    f32 = jnp.float32

    def to_plane(x):
        return lax.all_to_all(x, PLANE, split_axis=0, concat_axis=0, tiled=True)

    packed = normalize(tokens, norm_gain, routes, route_weight)
    weights = (w_gate[0], w_up[0], w_down[0])

    up2, down2 = from_line(packed, 2), from_line(packed, -2)
    up1, down1 = from_line(packed, 1), from_line(packed, -1)
    (up1, down1, up2, down2), held = lax.optimization_barrier(
        ((up1, down1, up2, down2), weights[1:])
    )
    across, up3, down3 = from_line(up2, 2), from_line(up2, 1), from_line(down2, -1)
    far_weights = [lax.ppermute(w, "c", [(0, 1), (1, 0)]) for w in (weights[0], *held)]

    own, own_half = (
        (
            (jnp.arange(places * n, dtype=jnp.int32) // n) * planes + lax.axis_index("z")
        ).astype(f32)[None]
        for n in (slots, slots // 2)
    )

    outgoing, near_scale, far_scale = dispatch(
        top, rows, width, own, own_half, packed, up1, down1, up2, down2, up3, across, down3
    )
    arrived = to_plane(outgoing)
    near_result, far_result = experts(arrived, (*weights, *far_weights))
    far_back = to_plane(far_result)
    far_back, near_result = lax.optimization_barrier((far_back, near_result))
    near_back = to_plane(near_result)
    flops = rows * gathered * width
    down2_far, up3, across, down3 = call(
        far_kernel,
        (shape(count, width, dtype=f32),) + (shape(count, width),) * 3,
        far_scale,
        far_back,
        limit=8,
        flops=flops,
    )
    across, up3, down3 = from_line(across, -2), from_line(up3, -1), from_line(down3, 1)
    own_sum, up1, down1, up2, down2 = call(
        near_kernel,
        (shape(count, width, dtype=f32),) + (shape(count, width),) * 4,
        near_scale,
        near_back,
        up3,
        across,
        down3,
        down2_far,
        limit=8,
        flops=flops,
    )
    up2, down2 = from_line(up2, -2), from_line(down2, 2)
    up1, down1 = from_line(up1, -1), from_line(down1, 1)
    layer_out = call(
        final_kernel, shape(count, width), tokens, own_sum, up1, down1, up2, down2, limit=4
    )
    return layer_out, attention(query_latent, query_rope, cache_latent, cache_rope, lengths)


def solution(mesh):
    split = Mesh(mesh.devices.reshape(2, 4, 2, 8, 2), ALL)
    return jax.shard_map(
        per_device,
        mesh=split,
        in_specs=(
            P(ALL, None),
            P(),
            P(ALL, None),
            P(ALL, None),
            P(EXPERT, None, "c"),
            P(EXPERT, None, "c"),
            P(EXPERT, "c", None),
            P(ALL, None, None),
            P(ALL, None, None),
            P(ALL, None, None),
            P(ALL, None, None),
            P(ALL),
        ),
        out_specs=(P(ALL, None), P(ALL, None, None)),
        check_vma=False,
    )
```

time: 147 us -> 121 us (0.82)
  waiting for transfers between devices: 37.1 us -> 21.3 us
  Pallas kernels: 27.7 us -> 14.4 us
  blocking collectives: 32 us -> 44.4 us
  local copies, waits for them, and re-layouts: 7.56 us -> 0.03 us
  other arithmetic: 2.95 us -> 0.34 us
  matrix products: 3.61 us -> 5.73 us
    all_to_all x1, waiting for transfers between devices: 24.2 us -> 0.01 us  [to_plane(): return lax.all_to_all(x, PLANE, split_axis=0, concat_axis=0, tiled=True)]
    all_to_all x1 -> x2, blocking collectives: 32 us -> 44.4 us  [to_plane(): return lax.all_to_all(x, PLANE, split_axis=0, concat_axis=0, tiled=True)]
    pallas_call x5 -> x3, Pallas kernels: 12.3 us -> 1.53 us  [call(): pl.pallas_call(kernel, out_shape=out_shape, scratch_shapes=scratch, compi...]
    ppermute x14, waiting for transfers between devices: 12.8 us -> 21.3 us  [from_line(): lax.ppermute(rows, 'z', [((i + distance) % planes, i) for i in range(plan...]
    unnamed x41 -> x10, local copies, waits for them, and re-layouts: 6.06 us -> 0.03 us
    pallas_call x1 -> x3, Pallas kernels: 15.3 us -> 12.8 us  [the longest x1 9.68 us: experts(): pl.pallas_call(expert_kernel, out_shape=[pltpu.HBM(half, rows.dtype)] * 2...]
    convert_element_type x4 -> x2, other arithmetic: 1.96 us -> 0.02 us  [per_device(): own, own_half = ((jnp.arange(places * n, dtype=jnp.int32) // n * planes +...]
  transfers between devices with their start and end apart: 18 -> 18, of which waited for: 8 -> 10; matrix products, arithmetic and copies ran while one was open for 3% -> 5% of each run, Pallas kernels for 1% -> 2%
where the time goes in v2:
time: 121 us; the launch traced here: 120 us
  blocking collectives  44.4 us (37%)
  starting transfers between devices  33.3 us (28%)
  waiting for transfers between devices  21.3 us (18%)
  Pallas kernels  14.4 us (12%)
  matrix products  5.73 us (5%)
    all_to_all x2, blocking collectives, to_plane(): return lax.all_to_all(x, PLANE, split_axis=0, concat_axis=0, tiled=True)  44.4 us
    ppermute x14, starting transfers between devices, from_line(): lax.ppermute(rows, 'z', [((i + distance) % planes, i) for i in range(plan...  27.5 us
    ppermute x14, waiting for transfers between devices, from_line(): lax.ppermute(rows, 'z', [((i + distance) % planes, i) for i in range(plan...  21.3 us
    pallas_call x1, Pallas kernels, experts(): pl.pallas_call(expert_kernel, out_shape=[pltpu.HBM(half, rows.dtype)] * 2...  9.68 us
    all_to_all x1, starting transfers between devices, to_plane(): return lax.all_to_all(x, PLANE, split_axis=0, concat_axis=0, tiled=True)  5.28 us
    dot_general x1, matrix products, attention(): jnp.einsum('rhp,rpl->rhl', probabilities, cache_latent, preferred_element...  3.03 us
  transfers between devices with their start and end apart: 18, of which 10 were waited for; matrix products, arithmetic and copies ran while one was open for 5% of the time, Pallas kernels for 2%

profile of v2, /device:TPU:6, one launch (start us, length us, event | category | flops | bytes accessed | tf_op | source)
XLA Modules:
  0.0 120.2 jit_solution(3333394241989773456)
XLA Ops:
  0.6 1.2 shard_map.131.refs_0_
  1.9 5.9 %collective-permute-start = (bf16[16,3712]{1,0:T(8,128)(2,1)S(1)}, bf16[16,3712]{1,0:T(8,128)(2,1)S(1)}, u32[]{:S(2)}, u32[]{:S(2)}) collective-permute-start(bf16[16,3712]{1,0:T(8,128)(2,1)S(1)} %shard_map.131.refs_0_), channel_id=1, source_target_pairs={{2,0},{4,2},{6,4},{8,6},{10,8},{12,10},{14,12},{0,14},{3,1},{5,3},... | collective-permute-start | bytes 356360 | tf_op jit(solution)/shard_map/ppermute | solution.py:292
  7.8 2.5 %collective-permute-start.2 = (bf16[16,3712]{1,0:T(8,128)(2,1)S(1)}, bf16[16,3712]{1,0:T(8,128)(2,1)S(1)}, u32[]{:S(2)}, u32[]{:S(2)}) collective-permute-start(bf16[16,3712]{1,0:T(8,128)(2,1)S(1)} %shard_map.131.refs_0_), channel_id=1, source_target_pairs={{4,0},{6,2},{8,4},{10,6},{12,8},{14,10},{0,12},{2,14},{5,1},{7,3},... | collective-permute-start | bytes 356360 | tf_op jit(solution)/shard_map/ppermute | solution.py:292
  10.9 2.9 %collective-permute-done.1.refs_2_ = bf16[16,3712]{1,0:T(8,128)(2,1)S(1)} collective-permute-done((bf16[16,3712]{1,0:T(8,128)(2,1)S(1)}, bf16[16,3712]{1,0:T(8,128)(2,1)S(1)}, u32[]{:S(2)}, u32[]{:S(2)}) %collective-permute-start.1) | collective-permute-done | bytes 118816 | tf_op jit(solution)/shard_map/ppermute | solution.py:292
  13.8 1.4 %collective-permute-done.2.refs_3_ = bf16[16,3712]{1,0:T(8,128)(2,1)S(1)} collective-permute-done((bf16[16,3712]{1,0:T(8,128)(2,1)S(1)}, bf16[16,3712]{1,0:T(8,128)(2,1)S(1)}, u32[]{:S(2)}, u32[]{:S(2)}) %collective-permute-start.2) | collective-permute-done | bytes 118816 | tf_op jit(solution)/shard_map/ppermute | solution.py:292
  15.3 3.8 %collective-permute-done.3.refs_4_ = bf16[16,3712]{1,0:T(8,128)(2,1)S(1)} collective-permute-done((bf16[16,3712]{1,0:T(8,128)(2,1)S(1)}, bf16[16,3712]{1,0:T(8,128)(2,1)S(1)}, u32[]{:S(2)}, u32[]{:S(2)}) %collective-permute-start.3) | collective-permute-done | bytes 118816 | tf_op jit(solution)/shard_map/ppermute | solution.py:292
  20.1 1.4 %collective-permute-start.5 = (bf16[16,3712]{1,0:T(8,128)(2,1)S(1)}, bf16[16,3712]{1,0:T(8,128)(2,1)S(1)}, u32[]{:S(2)}, u32[]{:S(2)}) collective-permute-start(bf16[16,3712]{1,0:T(8,128)(2,1)S(1)} %collective-permute-done.2.refs_3_), channel_id=1, source_target_pairs={{4,0},{6,2},{8,4},{10,6},{12,8},{14,10},{0,12},{2,14},{5,1},{7,3},... | collective-permute-start | bytes 356360 | tf_op jit(solution)/shard_map/ppermute | solution.py:292
  21.6 4.1 %collective-permute-done.4.refs_5_ = bf16[16,3712]{1,0:T(8,128)(2,1)S(1)} collective-permute-done((bf16[16,3712]{1,0:T(8,128)(2,1)S(1)}, bf16[16,3712]{1,0:T(8,128)(2,1)S(1)}, u32[]{:S(2)}, u32[]{:S(2)}) %collective-permute-start.4) | collective-permute-done | bytes 118816 | tf_op jit(solution)/shard_map/ppermute | solution.py:292
  25.6 4.2 %collective-permute-start.6 = (bf16[16,3712]{1,0:T(8,128)(2,1)S(1)}, bf16[16,3712]{1,0:T(8,128)(2,1)S(1)}, u32[]{:S(2)}, u32[]{:S(2)}) collective-permute-start(bf16[16,3712]{1,0:T(8,128)(2,1)S(1)} %collective-permute-done.3.refs_4_), channel_id=1, source_target_pairs={{14,0},{0,2},{2,4},{4,6},{6,8},{8,10},{10,12},{12,14},{15,1},{1,3}... | collective-permute-start | bytes 356360 | tf_op jit(solution)/shard_map/ppermute | solution.py:292
  29.9 1.0 collective-permute-done.5.refs_6_
  30.9 2.0 %collective-permute-done.6.refs_7_ = bf16[16,3712]{1,0:T(8,128)(2,1)S(1)} collective-permute-done((bf16[16,3712]{1,0:T(8,128)(2,1)S(1)}, bf16[16,3712]{1,0:T(8,128)(2,1)S(1)}, u32[]{:S(2)}, u32[]{:S(2)}) %collective-permute-start.6) | collective-permute-done | bytes 118816 | tf_op jit(solution)/shard_map/ppermute | solution.py:292
  32.8 2.0 %shard_map.132 = (bf16[256,3584]{1,0:T(8,128)(2,1)}, f32[64,128]{1,0:T(8,128)S(1)}, f32[64,128]{1,0:T(8,128)S(1)}) custom-call(f32[1,256]{1,0:T(1,128)S(1)} %fusion.8.own, f32[1,128]{1,0:T(1,128)S(1)} %fusion.11.own_half, bf16[16,3712]{1,0:T(8,128)(2,1)S(1)} %shard_map.131.refs_0_, bf16[16,3712]{1,0:T(8,128)(2,1)S(1)} %collective-permute-done.refs_1_, ...), custom_call_target="tpu_custom_call" | custom-call | flops 234881024 | bytes 3670016 | tf_op jit(solution)/shard_map/pallas_call | solution.py:168
  34.8 28.5 %all_to_all.34 = bf16[16,16,3584]{2,1,0:T(8,128)(2,1)S(1)} all-to-all(bf16[16,16,3584]{2,1,0:T(8,128)(2,1)} %bitcast.27), channel_id=1, replica_groups=mesh['xl'=2,'y'=4,'xh'=2,'z'=8,'c'=2] {'xl','y','xh'}, dimensions={0} | all-to-all | bytes 3670016 | tf_op jit(solution)/shard_map/all_to_all | solution.py:319
  63.3 9.7 %shard_map.133 = (bf16[128,3584]{1,0:T(8,128)(2,1)}, bf16[128,3584]{1,0:T(8,128)(2,1)}) custom-call(bf16[256,3584]{1,0:T(8,128)(2,1)S(1)} %bitcast.18, bf16[3584,512]{1,0:T(8,128)(2,1)} %bitcast.22, bf16[3584,512]{1,0:T(8,128)(2,1)} %bitcast.24, bf16[512,3584]{1,0:T(8,128)(2,1)} %bitcast.26, bf16[3584,512]{1,0:T(8,128)(2,1)} %collective-permute-done.7.refs_3_, ...), custom_call_target="tpu_custom_call" | custom-call | flops 5637144576 | bytes 22020096 | tf_op jit(solution)/shard_map/pallas_call | solution.py:269
  73.0 15.9 %all_to_all.35 = bf16[16,8,3584]{2,1,0:T(8,128)(2,1)S(1)} all-to-all(bf16[16,8,3584]{2,1,0:T(8,128)(2,1)} %bitcast.29), channel_id=1, replica_groups=mesh['xl'=2,'y'=4,'xh'=2,'z'=8,'c'=2] {'xl','y','xh'}, dimensions={0} | all-to-all | bytes 1835008 | tf_op jit(solution)/shard_map/all_to_all | solution.py:319
  88.9 5.3 %all-to-all-start.2 = ((bf16[16,8,3584]{2,1,0:T(8,128)(2,1)}), bf16[16,8,3584]{2,1,0:T(8,128)(2,1)S(1)}, u32[]{:S(2)}, u32[]{:S(2)}) async-start(bf16[16,8,3584]{2,1,0:T(8,128)(2,1)} %bitcast.28), calls=%async_computation.2 | async-start | bytes 1835008 | tf_op jit(solution)/shard_map/all_to_all | solution.py:319
  94.3 1.2 fusion.14
  95.5 1.5 %fusion.3 = f32[4,128,256]{2,1,0:T(8,128)S(1)} fusion(f32[4,128,256]{2,1,0:T(8,128)S(1)} %fusion.14, bf16[4,128,512]{2,1,0:T(8,128)(2,1)} %param.19, bf16[4,256,512]{2,1,0:T(8,128)(2,1)S(1)} %copy-done, pred[4,256]{1,0:T(4,128)(4,1)S(1)} %iota_compare_fusion), kind=kOutput, calls=%fused_computation.5 | convolution fusion | flops 134610944 | bytes 2622464 | tf_op jit(solution)/shard_map/rhl,rpl->rhp/dot_general | solution.py:20
  97.5 1.9 %collective-permute-start.10 = (bf16[16,3584]{1,0:T(8,128)(2,1)S(1)}, bf16[16,3584]{1,0:T(8,128)(2,1)S(1)}, u32[]{:S(2)}, u32[]{:S(2)}) collective-permute-start(bf16[16,3584]{1,0:T(8,128)(2,1)S(1)} %get-tuple-element.37), channel_id=1, source_target_pairs={{14,0},{0,2},{2,4},{4,6},{6,8},{8,10},{10,12},{12,14},{15,1},{1,3}... | collective-permute-start | bytes 344072 | tf_op jit(solution)/shard_map/ppermute | solution.py:292
  99.3 3.1 %collective-permute-start.12 = (bf16[16,3584]{1,0:T(8,128)(2,1)S(1)}, bf16[16,3584]{1,0:T(8,128)(2,1)S(1)}, u32[]{:S(2)}, u32[]{:S(2)}) collective-permute-start(bf16[16,3584]{1,0:T(8,128)(2,1)S(1)} %get-tuple-element.39), channel_id=1, source_target_pairs={{2,0},{4,2},{6,4},{8,6},{10,8},{12,10},{14,12},{0,14},{3,1},{5,3},... | collective-permute-start | bytes 344072 | tf_op jit(solution)/shard_map/ppermute | solution.py:292
  103.5 4.7 %collective-permute-done.11.across = bf16[16,3584]{1,0:T(8,128)(2,1)S(1)} collective-permute-done((bf16[16,3584]{1,0:T(8,128)(2,1)S(1)}, bf16[16,3584]{1,0:T(8,128)(2,1)S(1)}, u32[]{:S(2)}, u32[]{:S(2)}) %collective-permute-start.11) | collective-permute-done | bytes 114720 | tf_op jit(solution)/shard_map/ppermute | solution.py:292
  108.7 3.2 %collective-permute-start.14 = (bf16[16,3584]{1,0:T(8,128)(2,1)S(1)}, bf16[16,3584]{1,0:T(8,128)(2,1)S(1)}, u32[]{:S(2)}, u32[]{:S(2)}) collective-permute-start(bf16[16,3584]{1,0:T(8,128)(2,1)S(1)} %get-tuple-element.43), channel_id=1, source_target_pairs={{2,0},{4,2},{6,4},{8,6},{10,8},{12,10},{14,12},{0,14},{3,1},{5,3},... | collective-permute-start | bytes 344072 | tf_op jit(solution)/shard_map/ppermute | solution.py:292
  111.9 4.1 %collective-permute-start.16 = (bf16[16,3584]{1,0:T(8,128)(2,1)S(1)}, bf16[16,3584]{1,0:T(8,128)(2,1)S(1)}, u32[]{:S(2)}, u32[]{:S(2)}) collective-permute-start(bf16[16,3584]{1,0:T(8,128)(2,1)S(1)} %get-tuple-element.45), channel_id=1, source_target_pairs={{4,0},{6,2},{8,4},{10,6},{12,8},{14,10},{0,12},{2,14},{5,1},{7,3},... | collective-permute-start | bytes 344072 | tf_op jit(solution)/shard_map/ppermute | solution.py:292
  116.1 3.0 %convolution_convert_fusion = bf16[4,128,512]{2,1,0:T(8,128)(2,1)} fusion(bf16[4,256,512]{2,1,0:T(8,128)(2,1)S(1)} %copy-done, f32[4,128]{1,0:T(4,128)S(1)} %fusion.13, f32[4,128,256]{2,1,0:T(8,128)} %copy-done.2), kind=kOutput, calls=%fused_computation.1 | convolution fusion | flops 134873856 | bytes 2099200 | tf_op jit(solution)/shard_map/rhp,rpl->rhl/dot_general | solution.py:32
  (37 shorter events, 5.1 us)
Async XLA Ops:
  0.6 94.9 %copy-start = (bf16[4,256,512]{2,1,0:T(8,128)(2,1)S(1)}, bf16[4,256,512]{2,1,0:T(8,128)(2,1)}, u32[]{:S(2)}) copy-start(bf16[4,256,512]{2,1,0:T(8,128)(2,1)} %param.21) | copy-start | bytes 3145732
  1.9 9.1 %collective-permute-start = (bf16[16,3712]{1,0:T(8,128)(2,1)S(1)}, bf16[16,3712]{1,0:T(8,128)(2,1)S(1)}, u32[]{:S(2)}, u32[]{:S(2)}) collective-permute-start(bf16[16,3712]{1,0:T(8,128)(2,1)S(1)} %shard_map.131.refs_0_), channel_id=1, source_target_pairs={{2,0},{4,2},{6,4},{8,6},{10,8},{12,10},{14,12},{0,14},{3,1},{5,3},... | collective-permute-start | bytes 356360 | tf_op jit(solution)/shard_map/ppermute | solution.py:292
  7.8 6.0 %collective-permute-start.1 = (bf16[16,3712]{1,0:T(8,128)(2,1)S(1)}, bf16[16,3712]{1,0:T(8,128)(2,1)S(1)}, u32[]{:S(2)}, u32[]{:S(2)}) collective-permute-start(bf16[16,3712]{1,0:T(8,128)(2,1)S(1)} %shard_map.131.refs_0_), channel_id=1, source_target_pairs={{14,0},{0,2},{2,4},{4,6},{6,8},{8,10},{10,12},{12,14},{15,1},{1,3}... | collective-permute-start | bytes 356360 | tf_op jit(solution)/shard_map/ppermute | solution.py:292
  7.8 7.5 %collective-permute-start.2 = (bf16[16,3712]{1,0:T(8,128)(2,1)S(1)}, bf16[16,3712]{1,0:T(8,128)(2,1)S(1)}, u32[]{:S(2)}, u32[]{:S(2)}) collective-permute-start(bf16[16,3712]{1,0:T(8,128)(2,1)S(1)} %shard_map.131.refs_0_), channel_id=1, source_target_pairs={{4,0},{6,2},{8,4},{10,6},{12,8},{14,10},{0,12},{2,14},{5,1},{7,3},... | collective-permute-start | bytes 356360 | tf_op jit(solution)/shard_map/ppermute | solution.py:292
  10.3 8.8 %collective-permute-start.3 = (bf16[16,3712]{1,0:T(8,128)(2,1)S(1)}, bf16[16,3712]{1,0:T(8,128)(2,1)S(1)}, u32[]{:S(2)}, u32[]{:S(2)}) collective-permute-start(bf16[16,3712]{1,0:T(8,128)(2,1)S(1)} %shard_map.131.refs_0_), channel_id=1, source_target_pairs={{12,0},{14,2},{0,4},{2,6},{4,8},{6,10},{8,12},{10,14},{13,1},{15,3... | collective-permute-start | bytes 356360 | tf_op jit(solution)/shard_map/ppermute | solution.py:292
  10.7 52.6 %collective-permute-start.7 = (bf16[3584,512]{1,0:T(8,128)(2,1)}, bf16[3584,512]{1,0:T(8,128)(2,1)}, u32[]{:S(2)}, u32[]{:S(2)}) collective-permute-start(bf16[3584,512]{1,0:T(8,128)(2,1)} %bitcast.21), channel_id=1, source_target_pairs={{0,1},{1,0},{2,3},{3,2},{4,5},{5,4},{6,7},{7,6},{8,9},{9,8},{10,11... | collective-permute-start | bytes 11010056 | tf_op jit(solution)/shard_map/ppermute | solution.py:330
  19.0 44.3 %collective-permute-start.8 = (bf16[3584,512]{1,0:T(8,128)(2,1)}, bf16[3584,512]{1,0:T(8,128)(2,1)}, u32[]{:S(2)}, u32[]{:S(2)}) collective-permute-start(bf16[3584,512]{1,0:T(8,128)(2,1)} %bitcast.23), channel_id=1, source_target_pairs={{0,1},{1,0},{2,3},{3,2},{4,5},{5,4},{6,7},{7,6},{8,9},{9,8},{10,11... | collective-permute-start | bytes 11010056 | tf_op jit(solution)/shard_map/ppermute | solution.py:330
  19.0 44.3 %collective-permute-start.9 = (bf16[512,3584]{1,0:T(8,128)(2,1)}, bf16[512,3584]{1,0:T(8,128)(2,1)}, u32[]{:S(2)}, u32[]{:S(2)}) collective-permute-start(bf16[512,3584]{1,0:T(8,128)(2,1)} %bitcast.25), channel_id=1, source_target_pairs={{0,1},{1,0},{2,3},{3,2},{4,5},{5,4},{6,7},{7,6},{8,9},{9,8},{10,11... | collective-permute-start | bytes 11010056 | tf_op jit(solution)/shard_map/ppermute | solution.py:330
  19.5 6.1 %collective-permute-start.4 = (bf16[16,3712]{1,0:T(8,128)(2,1)S(1)}, bf16[16,3712]{1,0:T(8,128)(2,1)S(1)}, u32[]{:S(2)}, u32[]{:S(2)}) collective-permute-start(bf16[16,3712]{1,0:T(8,128)(2,1)S(1)} %collective-permute-done.2.refs_3_), channel_id=1, source_target_pairs={{2,0},{4,2},{6,4},{8,6},{10,8},{12,10},{14,12},{0,14},{3,1},{5,3},... | collective-permute-start | bytes 356360 | tf_op jit(solution)/shard_map/ppermute | solution.py:292
  20.1 10.7 %collective-permute-start.5 = (bf16[16,3712]{1,0:T(8,128)(2,1)S(1)}, bf16[16,3712]{1,0:T(8,128)(2,1)S(1)}, u32[]{:S(2)}, u32[]{:S(2)}) collective-permute-start(bf16[16,3712]{1,0:T(8,128)(2,1)S(1)} %collective-permute-done.2.refs_3_), channel_id=1, source_target_pairs={{4,0},{6,2},{8,4},{10,6},{12,8},{14,10},{0,12},{2,14},{5,1},{7,3},... | collective-permute-start | bytes 356360 | tf_op jit(solution)/shard_map/ppermute | solution.py:292
  25.6 7.2 %collective-permute-start.6 = (bf16[16,3712]{1,0:T(8,128)(2,1)S(1)}, bf16[16,3712]{1,0:T(8,128)(2,1)S(1)}, u32[]{:S(2)}, u32[]{:S(2)}) collective-permute-start(bf16[16,3712]{1,0:T(8,128)(2,1)S(1)} %collective-permute-done.3.refs_4_), channel_id=1, source_target_pairs={{14,0},{0,2},{2,4},{4,6},{6,8},{8,10},{10,12},{12,14},{15,1},{1,3}... | collective-permute-start | bytes 356360 | tf_op jit(solution)/shard_map/ppermute | solution.py:292
  73.0 21.2 %copy-start.4 = (s32[4]{0:T(128)S(1)}, s32[4]{0:T(128)}, u32[]{:S(2)}) copy-start(s32[4]{0:T(128)} %param.23) | copy-start | bytes 52
  73.0 21.3 %copy-start.3 = (bf16[4,128,64]{1,2,0:T(8,128)(2,1)S(1)}, bf16[4,128,64]{1,2,0:T(8,128)(2,1)}, u32[]{:S(2)}) copy-start(bf16[4,128,64]{1,2,0:T(8,128)(2,1)} %param.20) | copy-start | bytes 196612
  88.9 19.3 %all-to-all-start.2 = ((bf16[16,8,3584]{2,1,0:T(8,128)(2,1)}), bf16[16,8,3584]{2,1,0:T(8,128)(2,1)S(1)}, u32[]{:S(2)}, u32[]{:S(2)}) async-start(bf16[16,8,3584]{2,1,0:T(8,128)(2,1)} %bitcast.28), calls=%async_computation.2 | async-start | bytes 1835008 | tf_op jit(solution)/shard_map/all_to_all | solution.py:319
  97.0 11.2 %copy-start.2 = (f32[4,128,256]{2,1,0:T(8,128)}, f32[4,128,256]{2,1,0:T(8,128)S(1)}, u32[]{:S(2)}) copy-start(f32[4,128,256]{2,1,0:T(8,128)S(1)} %fusion.3) | copy-start | bytes 1572868
  97.0 22.5 %copy-start.1 = (bf16[16,3584]{1,0:T(8,128)(2,1)S(1)}, bf16[16,3584]{1,0:T(8,128)(2,1)}, u32[]{:S(2)}) copy-start(bf16[16,3584]{1,0:T(8,128)(2,1)} %tokens.1) | copy-start | bytes 344068
  97.5 6.1 %collective-permute-start.10 = (bf16[16,3584]{1,0:T(8,128)(2,1)S(1)}, bf16[16,3584]{1,0:T(8,128)(2,1)S(1)}, u32[]{:S(2)}, u32[]{:S(2)}) collective-permute-start(bf16[16,3584]{1,0:T(8,128)(2,1)S(1)} %get-tuple-element.37), channel_id=1, source_target_pairs={{14,0},{0,2},{2,4},{4,6},{6,8},{8,10},{10,12},{12,14},{15,1},{1,3}... | collective-permute-start | bytes 344072 | tf_op jit(solution)/shard_map/ppermute | solution.py:292
  99.3 8.9 %collective-permute-start.11 = (bf16[16,3584]{1,0:T(8,128)(2,1)S(1)}, bf16[16,3584]{1,0:T(8,128)(2,1)S(1)}, u32[]{:S(2)}, u32[]{:S(2)}) collective-permute-start(bf16[16,3584]{1,0:T(8,128)(2,1)S(1)} %get-tuple-element.38), channel_id=1, source_target_pairs={{12,0},{14,2},{0,4},{2,6},{4,8},{6,10},{8,12},{10,14},{13,1},{15,3... | collective-permute-start | bytes 344072 | tf_op jit(solution)/shard_map/ppermute | solution.py:292
  99.3 8.9 %collective-permute-start.12 = (bf16[16,3584]{1,0:T(8,128)(2,1)S(1)}, bf16[16,3584]{1,0:T(8,128)(2,1)S(1)}, u32[]{:S(2)}, u32[]{:S(2)}) collective-permute-start(bf16[16,3584]{1,0:T(8,128)(2,1)S(1)} %get-tuple-element.39), channel_id=1, source_target_pairs={{2,0},{4,2},{6,4},{8,6},{10,8},{12,10},{14,12},{0,14},{3,1},{5,3},... | collective-permute-start | bytes 344072 | tf_op jit(solution)/shard_map/ppermute | solution.py:292
  108.6 10.5 %collective-permute-start.13 = (bf16[16,3584]{1,0:T(8,128)(2,1)S(1)}, bf16[16,3584]{1,0:T(8,128)(2,1)S(1)}, u32[]{:S(2)}, u32[]{:S(2)}) collective-permute-start(bf16[16,3584]{1,0:T(8,128)(2,1)S(1)} %get-tuple-element.42), channel_id=1, source_target_pairs={{14,0},{0,2},{2,4},{4,6},{6,8},{8,10},{10,12},{12,14},{15,1},{1,3}... | collective-permute-start | bytes 344072 | tf_op jit(solution)/shard_map/ppermute | solution.py:292
  108.7 10.4 %collective-permute-start.14 = (bf16[16,3584]{1,0:T(8,128)(2,1)S(1)}, bf16[16,3584]{1,0:T(8,128)(2,1)S(1)}, u32[]{:S(2)}, u32[]{:S(2)}) collective-permute-start(bf16[16,3584]{1,0:T(8,128)(2,1)S(1)} %get-tuple-element.43), channel_id=1, source_target_pairs={{2,0},{4,2},{6,4},{8,6},{10,8},{12,10},{14,12},{0,14},{3,1},{5,3},... | collective-permute-start | bytes 344072 | tf_op jit(solution)/shard_map/ppermute | solution.py:292
  111.9 7.6 %collective-permute-start.15 = (bf16[16,3584]{1,0:T(8,128)(2,1)S(1)}, bf16[16,3584]{1,0:T(8,128)(2,1)S(1)}, u32[]{:S(2)}, u32[]{:S(2)}) collective-permute-start(bf16[16,3584]{1,0:T(8,128)(2,1)S(1)} %get-tuple-element.44), channel_id=1, source_target_pairs={{12,0},{14,2},{0,4},{2,6},{4,8},{6,10},{8,12},{10,14},{13,1},{15,3... | collective-permute-start | bytes 344072 | tf_op jit(solution)/shard_map/ppermute | solution.py:292
  111.9 7.6 %collective-permute-start.16 = (bf16[16,3584]{1,0:T(8,128)(2,1)S(1)}, bf16[16,3584]{1,0:T(8,128)(2,1)S(1)}, u32[]{:S(2)}, u32[]{:S(2)}) collective-permute-start(bf16[16,3584]{1,0:T(8,128)(2,1)S(1)} %get-tuple-element.45), channel_id=1, source_target_pairs={{4,0},{6,2},{8,4},{10,6},{12,8},{14,10},{0,12},{2,14},{5,1},{7,3},... | collective-permute-start | bytes 344072 | tf_op jit(solution)/shard_map/ppermute | solution.py:292

commit v3 on v2

--- a/solution.py
+++ b/solution.py
@@ -16,22 +16,70 @@
 MIB = 1024 * 1024
 
 
+def attention_kernel(lengths, latent_in, rope_in, cache_in, cache_rope_in, out, *scratch):
+    latent, rope, cache, cache_rope, built, sems, out_sems = scratch
+    requests, positions = cache.shape[0], cache.shape[1]
+    sources = (cache_in, latent_in, cache_rope_in, rope_in)
+    targets = (cache, latent, cache_rope, rope)
+    copies = [
+        [
+            pltpu.make_async_copy(source.at[r], target.at[r], sems.at[i, r])
+            for i, (source, target) in enumerate(zip(sources, targets))
+        ]
+        for r in range(requests)
+    ]
+    for group in copies:
+        for copy in group:
+            copy.start()
+    sent = []
+    for r in range(requests):
+        for copy in copies[r]:
+            copy.wait()
+        keys = cache[r]
+        scores = lax.dot_general(
+            latent[r], keys, (((1,), (1,)), ((), ())), preferred_element_type=jnp.float32
+        )
+        scores = (
+            scores
+            + lax.dot_general(
+                rope[r], cache_rope[r], (((0,), (0,)), ((), ())), preferred_element_type=jnp.float32
+            )
+        ) * score_scale
+        position = lax.broadcasted_iota(jnp.int32, scores.shape, 1)
+        scores = jnp.where(position < lengths[r], scores, -1e30)
+        weights = jnp.exp(scores - jnp.max(scores, axis=1, keepdims=True))
+        probabilities = weights / jnp.sum(weights, axis=1, keepdims=True)
+        built[r] = jnp.dot(
+            probabilities.astype(jnp.bfloat16), keys, preferred_element_type=jnp.float32
+        ).astype(jnp.bfloat16)
+        sent.append(pltpu.make_async_copy(built.at[r], out.at[r], out_sems.at[r]))
+        sent[-1].start()
+    for copy in sent:
+        copy.wait()
+
+
 def attention(query_latent, query_rope, cache_latent, cache_rope, lengths):
-    scores = jnp.einsum(
-        "rhl,rpl->rhp", query_latent, cache_latent, preferred_element_type=jnp.float32
-    )
-    scores = (
-        scores
-        + jnp.einsum("rhk,rkp->rhp", query_rope, cache_rope, preferred_element_type=jnp.float32)
-    ) * score_scale
-    in_range = jnp.arange(cache_latent.shape[1], dtype=jnp.int32)[None, :] < lengths[:, None]
-    scores = jnp.where(in_range[:, None, :], scores, -1e30)
-    highest = jnp.max(scores, axis=2, keepdims=True)
-    weights = jnp.exp(scores - highest)
-    probabilities = (weights / jnp.sum(weights, axis=2, keepdims=True)).astype(jnp.bfloat16)
-    return jnp.einsum(
-        "rhp,rpl->rhl", probabilities, cache_latent, preferred_element_type=jnp.float32
-    ).astype(jnp.bfloat16)
+    operands = (query_latent, jnp.swapaxes(query_rope, 1, 2), cache_latent, cache_rope)
+    requests = lengths.shape[0]
+    hbm = pl.BlockSpec(memory_space=pltpu.HBM)
+    return pl.pallas_call(
+        attention_kernel,
+        out_shape=pltpu.HBM(query_latent.shape, query_latent.dtype),
+        in_specs=[pl.BlockSpec(memory_space=pltpu.SMEM)] + [hbm] * 4,
+        out_specs=hbm,
+        scratch_shapes=[pltpu.VMEM(x.shape, x.dtype) for x in operands]
+        + [
+            pltpu.VMEM(query_latent.shape, query_latent.dtype),
+            pltpu.SemaphoreType.DMA((4, requests)),
+            pltpu.SemaphoreType.DMA((requests,)),
+        ],
+        compiler_params=pltpu.CompilerParams(vmem_limit_bytes=12 * MIB),
+        cost_estimate=pl.CostEstimate(
+            flops=4 * cache_latent.size * query_latent.shape[1],
+            bytes_accessed=4 * cache_latent.size,
+            transcendentals=0,
+        ),
+    )(lengths, *(in_hbm(x) for x in operands))
 
 
 def call(kernel, out_shape, *operands, limit, flops=0, scratch=()):
@@ -139,13 +187,12 @@
     return jnp.where(here, 1.0, 0.0), jnp.where(here, weight, 0.0)
 
 
-def dispatch_kernel(top, own, own_half, *refs):
-    blocks, (outgoing, near_scale, far_scale, built, sems) = refs[:-5], refs[-5:]
+def dispatch_kernel(top, own, *refs):
+    blocks, (outgoing, scale, built, sems) = refs[:-4], refs[-4:]
     count = blocks[0].shape[0]
-    half = count * len(blocks) // 2
     width = outgoing.shape[1]
     info = jnp.concatenate([b[:, width:] for b in blocks], axis=0).astype(jnp.float32)
-    place, _ = slots_of(info, own[...], count, top)
+    place, scale[...] = slots_of(info, own[...], count, top)
     place = place.astype(jnp.bfloat16)
     copies = []
     for i, start in enumerate(range(0, width, STEP)):
@@ -156,31 +203,30 @@
         ).astype(jnp.bfloat16)
         copies.append(pltpu.make_async_copy(built.at[:, cut], outgoing.at[:, cut], sems.at[i]))
         copies[-1].start()
-    _, near_scale[...] = slots_of(info[:half], own_half[...], count, top)
-    _, far_scale[...] = slots_of(info[half:], own_half[...], count, top)
     for copy in copies:
         copy.wait()
 
 
-def dispatch(top, rows, width, own, own_half, *blocks):
-    gathered = blocks[0].shape[0] * len(blocks)
-    any_vmem = pl.BlockSpec(memory_space=pltpu.VMEM)
+def dispatch(top, width, own, *blocks):
+    gathered, rows = blocks[0].shape[0] * len(blocks), own.shape[1]
     return pl.pallas_call(
         functools.partial(dispatch_kernel, top),
-        out_shape=[pltpu.HBM((rows, width), jnp.bfloat16)]
-        + [shape(gathered // 2, rows // 2, dtype=jnp.float32)] * 2,
-        out_specs=[pl.BlockSpec(memory_space=pltpu.HBM), any_vmem, any_vmem],
+        out_shape=[
+            pltpu.HBM((rows, width), jnp.bfloat16),
+            shape(gathered, rows, dtype=jnp.float32),
+        ],
+        out_specs=[pl.BlockSpec(memory_space=pltpu.HBM), pl.BlockSpec(memory_space=pltpu.VMEM)],
         scratch_shapes=[
             pltpu.VMEM((rows, width), jnp.bfloat16),
             pltpu.SemaphoreType.DMA((width // STEP,)),
         ],
-        compiler_params=pltpu.CompilerParams(vmem_limit_bytes=10 * MIB),
+        compiler_params=pltpu.CompilerParams(vmem_limit_bytes=8 * MIB),
         cost_estimate=pl.CostEstimate(
             flops=2 * rows * gathered * width,
             bytes_accessed=4 * rows * width,
             transcendentals=0,
         ),
-    )(own, own_half, *blocks)
+    )(own, *blocks)
 
 
 def weighted(scale, rows):
@@ -201,20 +247,18 @@
             block[:, cut] = sums[i * count : (i + 1) * count].astype(block.dtype)
 
 
-def near_kernel(scale, returned, up3, across, down3, down2_far, own, up1, down1, up2, down2):
+def near_kernel(scale, returned, up3, across, down3, own, up1, up2, down2):
     count, width = own.shape
     f32 = jnp.float32
-    step = 512
-    for start in range(0, width, step):
-        cut = slice(start, start + step)
+    for start in range(0, width, STEP):
+        cut = slice(start, start + STEP)
         sums = weighted(scale[...], returned[:, cut])
         own[:, cut] = sums[:count]
         up1[:, cut] = sums[count : 2 * count].astype(jnp.bfloat16)
-        down1[:, cut] = sums[2 * count : 3 * count].astype(jnp.bfloat16)
         up2[:, cut] = (
-            sums[3 * count :] + up3[:, cut].astype(f32) + across[:, cut].astype(f32)
+            sums[2 * count : 3 * count] + up3[:, cut].astype(f32) + across[:, cut].astype(f32)
         ).astype(jnp.bfloat16)
-    down2[...] = (down2_far[...] + down3[...].astype(f32)).astype(jnp.bfloat16)
+        down2[:, cut] = (sums[3 * count :] + down3[:, cut].astype(f32)).astype(jnp.bfloat16)
 
 
 def final_kernel(tokens, own, *refs):
@@ -224,14 +268,14 @@
     refs[-1][...] = (tokens[...].astype(jnp.float32) + total).astype(jnp.bfloat16)
 
 
-def expert_kernel(rows, *refs):
+def expert_kernel(near_rows, far_rows, *refs):
     weights, (near, far), held = refs[:6], refs[6:8], refs[8:14]
     near_built, far_built, total, sems, out_sems = refs[14:]
-    width = near.shape[1]
+    count, width = near.shape
     copies = [pltpu.make_async_copy(weights[i], held[i], sems.at[i]) for i in range(6)]
     for copy in copies:
         copy.start()
-    x = rows[...]
+    x = jnp.concatenate([near_rows[...], far_rows[...]], axis=0)
     sent = []
     for half in range(2):
         gate_copy, up_copy, down_copy = copies[3 * half : 3 * half + 3]
@@ -251,9 +295,8 @@
                 total[:, cut] = partial
                 continue
             sums = total[:, cut].astype(jnp.float32) + partial.astype(jnp.float32)
-            sums = sums.reshape(-1, 2, 8, STEP)
             for j, (built, out) in enumerate(((near_built, near), (far_built, far))):
-                built[:, cut] = sums[:, j].reshape(-1, STEP).astype(jnp.bfloat16)
+                built[:, cut] = sums[j * count : (j + 1) * count].astype(jnp.bfloat16)
                 sent.append(
                     pltpu.make_async_copy(built.at[:, cut], out.at[:, cut], out_sems.at[j, i])
                 )
@@ -262,19 +305,19 @@
         copy.wait()
 
 
-def experts(rows, weights):
-    count, width = rows.shape
+def experts(near_rows, far_rows, weights):
+    half, kind = near_rows.shape, near_rows.dtype
+    count, width = 2 * half[0], half[1]
     hbm = pl.BlockSpec(memory_space=pltpu.HBM)
-    half = (count // 2, width)
     return pl.pallas_call(
         expert_kernel,
-        out_shape=[pltpu.HBM(half, rows.dtype)] * 2,
-        in_specs=[pl.BlockSpec(memory_space=pltpu.VMEM)] + [hbm] * 6,
+        out_shape=[pltpu.HBM(half, kind)] * 2,
+        in_specs=[pl.BlockSpec(memory_space=pltpu.VMEM)] * 2 + [hbm] * 6,
         out_specs=[hbm] * 2,
         scratch_shapes=[pltpu.VMEM(w.shape, w.dtype) for w in weights]
-        + [pltpu.VMEM(half, rows.dtype)] * 2
+        + [pltpu.VMEM(half, kind)] * 2
         + [
-            pltpu.VMEM(rows.shape, rows.dtype),
+            pltpu.VMEM((count, width), kind),
             pltpu.SemaphoreType.DMA((6,)),
             pltpu.SemaphoreType.DMA((2, width // STEP)),
         ],
@@ -284,7 +327,7 @@
             bytes_accessed=2 * sum(w.size for w in weights),
             transcendentals=0,
         ),
-    )(rows, *(in_hbm(w) for w in weights))
+    )(near_rows, far_rows, *(in_hbm(w) for w in weights))
 
 
 def from_line(rows, distance):
@@ -310,9 +353,9 @@
     places = lax.axis_size(PLANE)
     count, top = routes.shape
     width = tokens.shape[1]
-    slots = 2 * planes
+    blocks = planes // 2
+    slots = 2 * blocks
     rows = places * slots
-    gathered = count * planes
     f32 = jnp.float32
 
     def to_plane(x):
@@ -323,55 +366,53 @@
 
     up2, down2 = from_line(packed, 2), from_line(packed, -2)
     up1, down1 = from_line(packed, 1), from_line(packed, -1)
-    (up1, down1, up2, down2), held = lax.optimization_barrier(
-        ((up1, down1, up2, down2), weights[1:])
+    (up2, down2, up1, down1), held = lax.optimization_barrier(
+        ((up2, down2, up1, down1), weights[1:])
     )
     across, up3, down3 = from_line(up2, 2), from_line(up2, 1), from_line(down2, -1)
     far_weights = [lax.ppermute(w, "c", [(0, 1), (1, 0)]) for w in (weights[0], *held)]
 
-    own, own_half = (
-        (
-            (jnp.arange(places * n, dtype=jnp.int32) // n) * planes + lax.axis_index("z")
-        ).astype(f32)[None]
-        for n in (slots, slots // 2)
-    )
-
-    outgoing, near_scale, far_scale = dispatch(
-        top, rows, width, own, own_half, packed, up1, down1, up2, down2, up3, across, down3
-    )
-    arrived = to_plane(outgoing)
-    near_result, far_result = experts(arrived, (*weights, *far_weights))
+    own = (
+        (jnp.arange(rows, dtype=jnp.int32) // slots) * planes + lax.axis_index("z")
+    ).astype(f32)[None]
+    near, near_scale = dispatch(top, width, own, packed, up1, up2, down2)
+    far, far_scale = dispatch(top, width, own, down1, up3, across, down3)
+    near_rows = to_plane(near)
+    near_rows, far = lax.optimization_barrier((near_rows, far))
+    far_rows = to_plane(far)
+    near_result, far_result = experts(near_rows, far_rows, (*weights, *far_weights))
     far_back = to_plane(far_result)
+    attended = attention(query_latent, query_rope, cache_latent, cache_rope, lengths)
     far_back, near_result = lax.optimization_barrier((far_back, near_result))
     near_back = to_plane(near_result)
-    flops = rows * gathered * width
-    down2_far, up3, across, down3 = call(
+    flops = 4 * rows * count * blocks * width
+    down1, up3, across, down3 = call(
         far_kernel,
-        (shape(count, width, dtype=f32),) + (shape(count, width),) * 3,
+        (shape(count, width),) * 4,
         far_scale,
         far_back,
         limit=8,
         flops=flops,
     )
     across, up3, down3 = from_line(across, -2), from_line(up3, -1), from_line(down3, 1)
-    own_sum, up1, down1, up2, down2 = call(
+    down1 = from_line(down1, 1)
+    up3, across, down3, attended = lax.optimization_barrier((up3, across, down3, attended))
+    own_sum, up1, up2, down2 = call(
         near_kernel,
-        (shape(count, width, dtype=f32),) + (shape(count, width),) * 4,
+        (shape(count, width, dtype=f32),) + (shape(count, width),) * 3,
         near_scale,
         near_back,
         up3,
         across,
         down3,
-        down2_far,
         limit=8,
         flops=flops,
     )
-    up2, down2 = from_line(up2, -2), from_line(down2, 2)
-    up1, down1 = from_line(up1, -1), from_line(down1, 1)
+    up2, down2, up1 = from_line(up2, -2), from_line(down2, 2), from_line(up1, -1)
     layer_out = call(
-        final_kernel, shape(count, width), tokens, own_sum, up1, down1, up2, down2, limit=4
-    )
-    return layer_out, attention(query_latent, query_rope, cache_latent, cache_rope, lengths)
+        final_kernel, shape(count, width), tokens, own_sum, up2, down2, up1, down1, limit=4
+    )
+    return layer_out, attended
 
 
 def solution(mesh):

time: 121 us -> 115 us (0.950)
  blocking collectives: 44.4 us -> 33.4 us
  Pallas kernels: 14.4 us -> 20.3 us
  matrix products: 5.73 us -> 0 us
  waiting for transfers between devices: 21.3 us -> 25.3 us
    all_to_all x2, blocking collectives: 44.4 us -> 33.4 us  [to_plane(): return lax.all_to_all(x, PLANE, split_axis=0, concat_axis=0, tiled=True)]
    all_to_all x1 -> x2, starting transfers between devices: 5.28 us -> 12.7 us  [to_plane(): return lax.all_to_all(x, PLANE, split_axis=0, concat_axis=0, tiled=True)]
    ppermute x14, starting transfers between devices: 27.5 us -> 21.2 us  [from_line(): lax.ppermute(rows, 'z', [((i + distance) % planes, i) for i in range(plan...]
    dot_general x3 -> x0, matrix products: 5.73 us -> none  [the longest x1 3.03 us: attention(): jnp.einsum('rhp,rpl->rhl', probabilities, cache_latent, preferred_element...]
    pallas_call x1 -> x2, Pallas kernels: 9.68 us -> 14.7 us  [the longest x1 9.62 us: experts(): pl.pallas_call(expert_kernel, out_shape=[pltpu.HBM(half, kind)] * 2, in_s...]
    ppermute x14, waiting for transfers between devices: 21.3 us -> 25.2 us  [from_line(): lax.ppermute(rows, 'z', [((i + distance) % planes, i) for i in range(plan...]
    pallas_call x1 -> x2, Pallas kernels: 1.96 us -> 2.99 us  [dispatch(): pl.pallas_call(functools.partial(dispatch_kernel, top), out_shape=[pltpu....]
  transfers between devices with their start and end apart: 18 -> 19, of which waited for: 10 -> 8; matrix products, arithmetic and copies ran while one was open for 5% -> 0% of each run, Pallas kernels for 2% -> 8%
where the time goes in v3:
time: 115 us; the launch traced here: 114 us
  starting transfers between devices  34.3 us (30%)
  blocking collectives  33.4 us (29%)
  waiting for transfers between devices  25.3 us (22%)
  Pallas kernels  20.3 us (18%)
    all_to_all x2, blocking collectives, to_plane(): return lax.all_to_all(x, PLANE, split_axis=0, concat_axis=0, tiled=True)  33.4 us
    ppermute x14, waiting for transfers between devices, from_line(): lax.ppermute(rows, 'z', [((i + distance) % planes, i) for i in range(plan...  25.2 us
    ppermute x14, starting transfers between devices, from_line(): lax.ppermute(rows, 'z', [((i + distance) % planes, i) for i in range(plan...  21.2 us
    all_to_all x2, starting transfers between devices, to_plane(): return lax.all_to_all(x, PLANE, split_axis=0, concat_axis=0, tiled=True)  12.7 us
    pallas_call x1, Pallas kernels, experts(): pl.pallas_call(expert_kernel, out_shape=[pltpu.HBM(half, kind)] * 2, in_s...  9.62 us
    pallas_call x1, Pallas kernels, attention(): pl.pallas_call(attention_kernel, out_shape=pltpu.HBM(query_latent.shape,...  5.04 us
    pallas_call x2, Pallas kernels, dispatch(): pl.pallas_call(functools.partial(dispatch_kernel, top), out_shape=[pltpu....  2.99 us
  transfers between devices with their start and end apart: 19, of which 8 were waited for; matrix products, arithmetic and copies ran while one was open for 0% of the time, Pallas kernels for 8%

profile of v3, /device:TPU:6, one launch (start us, length us, event | category | flops | bytes accessed | tf_op | source)
XLA Modules:
  0.0 114.1 jit_solution(12854127445102099082)
XLA Ops:
  0.6 1.1 shard_map.131.refs_0_
  1.7 6.4 %collective-permute-start = (bf16[16,3712]{1,0:T(8,128)(2,1)S(1)}, bf16[16,3712]{1,0:T(8,128)(2,1)S(1)}, u32[]{:S(2)}, u32[]{:S(2)}) collective-permute-start(bf16[16,3712]{1,0:T(8,128)(2,1)S(1)} %shard_map.131.refs_0_), channel_id=1, source_target_pairs={{4,0},{6,2},{8,4},{10,6},{12,8},{14,10},{0,12},{2,14},{5,1},{7,3},... | collective-permute-start | bytes 356360 | tf_op jit(solution)/shard_map/ppermute | solution.py:335
  8.1 3.7 %collective-permute-start.2 = (bf16[16,3712]{1,0:T(8,128)(2,1)S(1)}, bf16[16,3712]{1,0:T(8,128)(2,1)S(1)}, u32[]{:S(2)}, u32[]{:S(2)}) collective-permute-start(bf16[16,3712]{1,0:T(8,128)(2,1)S(1)} %shard_map.131.refs_0_), channel_id=1, source_target_pairs={{2,0},{4,2},{6,4},{8,6},{10,8},{12,10},{14,12},{0,14},{3,1},{5,3},... | collective-permute-start | bytes 356360 | tf_op jit(solution)/shard_map/ppermute | solution.py:335
  11.8 2.1 %collective-permute-done.refs_2_ = bf16[16,3712]{1,0:T(8,128)(2,1)S(1)} collective-permute-done((bf16[16,3712]{1,0:T(8,128)(2,1)S(1)}, bf16[16,3712]{1,0:T(8,128)(2,1)S(1)}, u32[]{:S(2)}, u32[]{:S(2)}) %collective-permute-start) | collective-permute-done | bytes 118816 | tf_op jit(solution)/shard_map/ppermute | solution.py:335
  14.0 4.0 %collective-permute-done.1.refs_3_ = bf16[16,3712]{1,0:T(8,128)(2,1)S(1)} collective-permute-done((bf16[16,3712]{1,0:T(8,128)(2,1)S(1)}, bf16[16,3712]{1,0:T(8,128)(2,1)S(1)}, u32[]{:S(2)}, u32[]{:S(2)}) %collective-permute-start.1) | collective-permute-done | bytes 118816 | tf_op jit(solution)/shard_map/ppermute | solution.py:335
  18.0 1.6 %collective-permute-done.3.refs_0_ = bf16[16,3712]{1,0:T(8,128)(2,1)S(1)} collective-permute-done((bf16[16,3712]{1,0:T(8,128)(2,1)S(1)}, bf16[16,3712]{1,0:T(8,128)(2,1)S(1)}, u32[]{:S(2)}, u32[]{:S(2)}) %collective-permute-start.3) | collective-permute-done | bytes 118816 | tf_op jit(solution)/shard_map/ppermute | solution.py:335
  20.1 1.5 %shard_map.132 = (bf16[128,3584]{1,0:T(8,128)(2,1)}, f32[64,128]{1,0:T(8,128)S(1)}) custom-call(f32[1,128]{1,0:T(1,128)S(1)} %fusion.2.own, bf16[16,3712]{1,0:T(8,128)(2,1)S(1)} %shard_map.131.refs_0_, bf16[16,3712]{1,0:T(8,128)(2,1)S(1)} %collective-permute-done.2.refs_1_, bf16[16,3712]{1,0:T(8,128)(2,1)S(1)} %collective-permute-done.refs_2_, ...), custom_call_target="tpu_custom_call" | custom-call | flops 58720256 | bytes 1835008 | tf_op jit(solution)/shard_map/pallas_call | solution.py:212
  21.6 7.4 %all-to-all-start = ((bf16[16,8,3584]{2,1,0:T(8,128)(2,1)}), bf16[16,8,3584]{2,1,0:T(8,128)(2,1)S(1)}, u32[]{:S(2)}, u32[]{:S(2)}) async-start(bf16[16,8,3584]{2,1,0:T(8,128)(2,1)} %bitcast.25), calls=%async_computation | async-start | bytes 1835008 | tf_op jit(solution)/shard_map/all_to_all | solution.py:362
  29.5 0.8 collective-permute-start.5
  30.3 6.1 %collective-permute-done.4.refs_1_ = bf16[16,3712]{1,0:T(8,128)(2,1)S(1)} collective-permute-done((bf16[16,3712]{1,0:T(8,128)(2,1)S(1)}, bf16[16,3712]{1,0:T(8,128)(2,1)S(1)}, u32[]{:S(2)}, u32[]{:S(2)}) %collective-permute-start.4) | collective-permute-done | bytes 118816 | tf_op jit(solution)/shard_map/ppermute | solution.py:335
  36.4 1.4 %collective-permute-done.5.refs_2_ = bf16[16,3712]{1,0:T(8,128)(2,1)S(1)} collective-permute-done((bf16[16,3712]{1,0:T(8,128)(2,1)S(1)}, bf16[16,3712]{1,0:T(8,128)(2,1)S(1)}, u32[]{:S(2)}, u32[]{:S(2)}) %collective-permute-start.5) | collective-permute-done | bytes 118816 | tf_op jit(solution)/shard_map/ppermute | solution.py:335
  37.8 4.7 %collective-permute-done.6.refs_3_ = bf16[16,3712]{1,0:T(8,128)(2,1)S(1)} collective-permute-done((bf16[16,3712]{1,0:T(8,128)(2,1)S(1)}, bf16[16,3712]{1,0:T(8,128)(2,1)S(1)}, u32[]{:S(2)}, u32[]{:S(2)}) %collective-permute-start.6) | collective-permute-done | bytes 118816 | tf_op jit(solution)/shard_map/ppermute | solution.py:335
  42.4 1.5 %shard_map.133 = (bf16[128,3584]{1,0:T(8,128)(2,1)}, f32[64,128]{1,0:T(8,128)S(1)}) custom-call(f32[1,128]{1,0:T(1,128)S(1)} %fusion.2.own, bf16[16,3712]{1,0:T(8,128)(2,1)S(1)} %collective-permute-done.3.refs_0_, bf16[16,3712]{1,0:T(8,128)(2,1)S(1)} %collective-permute-done.4.refs_1_, bf16[16,3712]{1,0:T(8,128)(2,1)S(1)} %collective-permute-done.5.refs_2_, ...), custom_call_target="tpu_custom_call" | custom-call | flops 58720256 | bytes 1835008 | tf_op jit(solution)/shard_map/pallas_call | solution.py:212
  44.0 17.7 %all_to_all.46 = bf16[16,8,3584]{2,1,0:T(8,128)(2,1)S(1)} all-to-all(bf16[16,8,3584]{2,1,0:T(8,128)(2,1)} %bitcast.26), channel_id=1, replica_groups=mesh['xl'=2,'y'=4,'xh'=2,'z'=8,'c'=2] {'xl','y','xh'}, dimensions={0} | all-to-all | bytes 1835008 | tf_op jit(solution)/shard_map/all_to_all | solution.py:362
  61.7 9.6 %shard_map.134 = (bf16[128,3584]{1,0:T(8,128)(2,1)}, bf16[128,3584]{1,0:T(8,128)(2,1)}) custom-call(bf16[128,3584]{1,0:T(8,128)(2,1)S(1)} %bitcast.16, bf16[128,3584]{1,0:T(8,128)(2,1)S(1)} %bitcast.17, bf16[3584,512]{1,0:T(8,128)(2,1)} %bitcast.19, bf16[3584,512]{1,0:T(8,128)(2,1)} %bitcast.21, bf16[512,3584]{1,0:T(8,128)(2,1)} %bitcast.23, ...), custom_call_target="tpu_custom_call" | custom-call | flops 5637144576 | bytes 22020096 | tf_op jit(solution)/shard_map/pallas_call | solution.py:312
  71.3 15.7 %all_to_all.47 = bf16[16,8,3584]{2,1,0:T(8,128)(2,1)S(1)} all-to-all(bf16[16,8,3584]{2,1,0:T(8,128)(2,1)} %bitcast.27), channel_id=1, replica_groups=mesh['xl'=2,'y'=4,'xh'=2,'z'=8,'c'=2] {'xl','y','xh'}, dimensions={0} | all-to-all | bytes 1835008 | tf_op jit(solution)/shard_map/all_to_all | solution.py:362
  87.1 5.2 %all-to-all-start.3 = ((bf16[16,8,3584]{2,1,0:T(8,128)(2,1)}), bf16[16,8,3584]{2,1,0:T(8,128)(2,1)S(1)}, u32[]{:S(2)}, u32[]{:S(2)}) async-start(bf16[16,8,3584]{2,1,0:T(8,128)(2,1)} %bitcast.24), calls=%async_computation.3 | async-start | bytes 1835008 | tf_op jit(solution)/shard_map/all_to_all | solution.py:362
  93.1 3.1 %collective-permute-start.12 = (bf16[16,3584]{1,0:T(8,128)(2,1)S(1)}, bf16[16,3584]{1,0:T(8,128)(2,1)S(1)}, u32[]{:S(2)}, u32[]{:S(2)}) collective-permute-start(bf16[16,3584]{1,0:T(8,128)(2,1)S(1)} %get-tuple-element.48), channel_id=1, source_target_pairs={{2,0},{4,2},{6,4},{8,6},{10,8},{12,10},{14,12},{0,14},{3,1},{5,3},... | collective-permute-start | bytes 344072 | tf_op jit(solution)/shard_map/ppermute | solution.py:335
  96.2 5.0 %shard_map.136 = bf16[4,128,512]{2,1,0:T(8,128)(2,1)} custom-call(s32[4]{0:T(128)S(1)} %copy-done.1, bf16[4,128,512]{2,1,0:T(8,128)(2,1)} %latent_in.1, bf16[4,64,128]{2,1,0:T(8,128)(2,1)} %bitcast.28, bf16[4,256,512]{2,1,0:T(8,128)(2,1)} %cache_in.1, bf16[4,64,256]{2,1,0:T(8,128)(2,1)} %cache_rope_in.1), custom_call_target="tpu_custom_call" | custom-call | flops 268435456 | bytes 2097152 | tf_op jit(solution)/shard_map/pallas_call | solution.py:65
  101.3 1.4 %collective-permute-start.16 = (bf16[16,3584]{1,0:T(8,128)(2,1)S(1)}, bf16[16,3584]{1,0:T(8,128)(2,1)S(1)}, u32[]{:S(2)}, u32[]{:S(2)}) collective-permute-start(bf16[16,3584]{1,0:T(8,128)(2,1)S(1)} %get-tuple-element.56), channel_id=1, source_target_pairs={{2,0},{4,2},{6,4},{8,6},{10,8},{12,10},{14,12},{0,14},{3,1},{5,3},... | collective-permute-start | bytes 344072 | tf_op jit(solution)/shard_map/ppermute | solution.py:335
  103.3 4.0 %collective-permute-start.14 = (bf16[16,3584]{1,0:T(8,128)(2,1)S(1)}, bf16[16,3584]{1,0:T(8,128)(2,1)S(1)}, u32[]{:S(2)}, u32[]{:S(2)}) collective-permute-start(bf16[16,3584]{1,0:T(8,128)(2,1)S(1)} %get-tuple-element.54), channel_id=1, source_target_pairs={{4,0},{6,2},{8,4},{10,6},{12,8},{14,10},{0,12},{2,14},{5,1},{7,3},... | collective-permute-start | bytes 344072 | tf_op jit(solution)/shard_map/ppermute | solution.py:335
  108.0 3.3 %collective-permute-done.13.refs_0_ = bf16[16,3584]{1,0:T(8,128)(2,1)S(1)} collective-permute-done((bf16[16,3584]{1,0:T(8,128)(2,1)S(1)}, bf16[16,3584]{1,0:T(8,128)(2,1)S(1)}, u32[]{:S(2)}, u32[]{:S(2)}) %collective-permute-start.13) | collective-permute-done | bytes 114720 | tf_op jit(solution)/shard_map/ppermute | solution.py:335
  111.3 2.0 %collective-permute-done.15.refs_2_ = bf16[16,3584]{1,0:T(8,128)(2,1)S(1)} collective-permute-done((bf16[16,3584]{1,0:T(8,128)(2,1)S(1)}, bf16[16,3584]{1,0:T(8,128)(2,1)S(1)}, u32[]{:S(2)}, u32[]{:S(2)}) %collective-permute-start.15) | collective-permute-done | bytes 114720 | tf_op jit(solution)/shard_map/ppermute | solution.py:335
  113.3 0.7 shard_map.138
  (29 shorter events, 3.0 us)
Async XLA Ops:
  1.7 12.2 %collective-permute-start = (bf16[16,3712]{1,0:T(8,128)(2,1)S(1)}, bf16[16,3712]{1,0:T(8,128)(2,1)S(1)}, u32[]{:S(2)}, u32[]{:S(2)}) collective-permute-start(bf16[16,3712]{1,0:T(8,128)(2,1)S(1)} %shard_map.131.refs_0_), channel_id=1, source_target_pairs={{4,0},{6,2},{8,4},{10,6},{12,8},{14,10},{0,12},{2,14},{5,1},{7,3},... | collective-permute-start | bytes 356360 | tf_op jit(solution)/shard_map/ppermute | solution.py:335
  8.1 9.9 %collective-permute-start.1 = (bf16[16,3712]{1,0:T(8,128)(2,1)S(1)}, bf16[16,3712]{1,0:T(8,128)(2,1)S(1)}, u32[]{:S(2)}, u32[]{:S(2)}) collective-permute-start(bf16[16,3712]{1,0:T(8,128)(2,1)S(1)} %shard_map.131.refs_0_), channel_id=1, source_target_pairs={{12,0},{14,2},{0,4},{2,6},{4,8},{6,10},{8,12},{10,14},{13,1},{15,3... | collective-permute-start | bytes 356360 | tf_op jit(solution)/shard_map/ppermute | solution.py:335
  8.1 9.9 %collective-permute-start.2 = (bf16[16,3712]{1,0:T(8,128)(2,1)S(1)}, bf16[16,3712]{1,0:T(8,128)(2,1)S(1)}, u32[]{:S(2)}, u32[]{:S(2)}) collective-permute-start(bf16[16,3712]{1,0:T(8,128)(2,1)S(1)} %shard_map.131.refs_0_), channel_id=1, source_target_pairs={{2,0},{4,2},{6,4},{8,6},{10,8},{12,10},{14,12},{0,14},{3,1},{5,3},... | collective-permute-start | bytes 356360 | tf_op jit(solution)/shard_map/ppermute | solution.py:335
  11.8 7.8 %collective-permute-start.3 = (bf16[16,3712]{1,0:T(8,128)(2,1)S(1)}, bf16[16,3712]{1,0:T(8,128)(2,1)S(1)}, u32[]{:S(2)}, u32[]{:S(2)}) collective-permute-start(bf16[16,3712]{1,0:T(8,128)(2,1)S(1)} %shard_map.131.refs_0_), channel_id=1, source_target_pairs={{14,0},{0,2},{2,4},{4,6},{6,8},{8,10},{10,12},{12,14},{15,1},{1,3}... | collective-permute-start | bytes 356360 | tf_op jit(solution)/shard_map/ppermute | solution.py:335
  11.8 49.9 %collective-permute-start.7 = (bf16[3584,512]{1,0:T(8,128)(2,1)}, bf16[3584,512]{1,0:T(8,128)(2,1)}, u32[]{:S(2)}, u32[]{:S(2)}) collective-permute-start(bf16[3584,512]{1,0:T(8,128)(2,1)} %bitcast.18), channel_id=1, source_target_pairs={{0,1},{1,0},{2,3},{3,2},{4,5},{5,4},{6,7},{7,6},{8,9},{9,8},{10,11... | collective-permute-start | bytes 11010056 | tf_op jit(solution)/shard_map/ppermute | solution.py:373
  19.6 42.1 %collective-permute-start.8 = (bf16[3584,512]{1,0:T(8,128)(2,1)}, bf16[3584,512]{1,0:T(8,128)(2,1)}, u32[]{:S(2)}, u32[]{:S(2)}) collective-permute-start(bf16[3584,512]{1,0:T(8,128)(2,1)} %bitcast.20), channel_id=1, source_target_pairs={{0,1},{1,0},{2,3},{3,2},{4,5},{5,4},{6,7},{7,6},{8,9},{9,8},{10,11... | collective-permute-start | bytes 11010056 | tf_op jit(solution)/shard_map/ppermute | solution.py:373
  19.6 42.1 %collective-permute-start.9 = (bf16[512,3584]{1,0:T(8,128)(2,1)}, bf16[512,3584]{1,0:T(8,128)(2,1)}, u32[]{:S(2)}, u32[]{:S(2)}) collective-permute-start(bf16[512,3584]{1,0:T(8,128)(2,1)} %bitcast.22), channel_id=1, source_target_pairs={{0,1},{1,0},{2,3},{3,2},{4,5},{5,4},{6,7},{7,6},{8,9},{9,8},{10,11... | collective-permute-start | bytes 11010056 | tf_op jit(solution)/shard_map/ppermute | solution.py:373
  21.6 22.4 %all-to-all-start = ((bf16[16,8,3584]{2,1,0:T(8,128)(2,1)}), bf16[16,8,3584]{2,1,0:T(8,128)(2,1)S(1)}, u32[]{:S(2)}, u32[]{:S(2)}) async-start(bf16[16,8,3584]{2,1,0:T(8,128)(2,1)} %bitcast.25), calls=%async_computation | async-start | bytes 1835008 | tf_op jit(solution)/shard_map/all_to_all | solution.py:362
  29.0 7.4 %collective-permute-start.4 = (bf16[16,3712]{1,0:T(8,128)(2,1)S(1)}, bf16[16,3712]{1,0:T(8,128)(2,1)S(1)}, u32[]{:S(2)}, u32[]{:S(2)}) collective-permute-start(bf16[16,3712]{1,0:T(8,128)(2,1)S(1)} %collective-permute-done.refs_2_), channel_id=1, source_target_pairs={{2,0},{4,2},{6,4},{8,6},{10,8},{12,10},{14,12},{0,14},{3,1},{5,3},... | collective-permute-start | bytes 356360 | tf_op jit(solution)/shard_map/ppermute | solution.py:335
  29.5 8.3 %collective-permute-start.5 = (bf16[16,3712]{1,0:T(8,128)(2,1)S(1)}, bf16[16,3712]{1,0:T(8,128)(2,1)S(1)}, u32[]{:S(2)}, u32[]{:S(2)}) collective-permute-start(bf16[16,3712]{1,0:T(8,128)(2,1)S(1)} %collective-permute-done.refs_2_), channel_id=1, source_target_pairs={{4,0},{6,2},{8,4},{10,6},{12,8},{14,10},{0,12},{2,14},{5,1},{7,3},... | collective-permute-start | bytes 356360 | tf_op jit(solution)/shard_map/ppermute | solution.py:335
  36.4 6.0 %collective-permute-start.6 = (bf16[16,3712]{1,0:T(8,128)(2,1)S(1)}, bf16[16,3712]{1,0:T(8,128)(2,1)S(1)}, u32[]{:S(2)}, u32[]{:S(2)}) collective-permute-start(bf16[16,3712]{1,0:T(8,128)(2,1)S(1)} %collective-permute-done.1.refs_3_), channel_id=1, source_target_pairs={{14,0},{0,2},{2,4},{4,6},{6,8},{8,10},{10,12},{12,14},{15,1},{1,3}... | collective-permute-start | bytes 356360 | tf_op jit(solution)/shard_map/ppermute | solution.py:335
  71.3 24.9 %copy-start.1 = (s32[4]{0:T(128)S(1)}, s32[4]{0:T(128)}, u32[]{:S(2)}) copy-start(s32[4]{0:T(128)} %lengths.1) | copy-start | bytes 52
  71.3 42.0 %copy-start = (bf16[16,3584]{1,0:T(8,128)(2,1)S(1)}, bf16[16,3584]{1,0:T(8,128)(2,1)}, u32[]{:S(2)}) copy-start(bf16[16,3584]{1,0:T(8,128)(2,1)} %tokens.1) | copy-start | bytes 344068
  87.1 15.6 %all-to-all-start.3 = ((bf16[16,8,3584]{2,1,0:T(8,128)(2,1)}), bf16[16,8,3584]{2,1,0:T(8,128)(2,1)S(1)}, u32[]{:S(2)}, u32[]{:S(2)}) async-start(bf16[16,8,3584]{2,1,0:T(8,128)(2,1)} %bitcast.24), calls=%async_computation.3 | async-start | bytes 1835008 | tf_op jit(solution)/shard_map/all_to_all | solution.py:362
  92.7 10.0 %collective-permute-start.10 = (bf16[16,3584]{1,0:T(8,128)(2,1)S(1)}, bf16[16,3584]{1,0:T(8,128)(2,1)S(1)}, u32[]{:S(2)}, u32[]{:S(2)}) collective-permute-start(bf16[16,3584]{1,0:T(8,128)(2,1)S(1)} %get-tuple-element.46), channel_id=1, source_target_pairs={{14,0},{0,2},{2,4},{4,6},{6,8},{8,10},{10,12},{12,14},{15,1},{1,3}... | collective-permute-start | bytes 344072 | tf_op jit(solution)/shard_map/ppermute | solution.py:335
  92.8 9.9 %collective-permute-start.11 = (bf16[16,3584]{1,0:T(8,128)(2,1)S(1)}, bf16[16,3584]{1,0:T(8,128)(2,1)S(1)}, u32[]{:S(2)}, u32[]{:S(2)}) collective-permute-start(bf16[16,3584]{1,0:T(8,128)(2,1)S(1)} %get-tuple-element.47), channel_id=1, source_target_pairs={{12,0},{14,2},{0,4},{2,6},{4,8},{6,10},{8,12},{10,14},{13,1},{15,3... | collective-permute-start | bytes 344072 | tf_op jit(solution)/shard_map/ppermute | solution.py:335
  93.1 9.6 %collective-permute-start.12 = (bf16[16,3584]{1,0:T(8,128)(2,1)S(1)}, bf16[16,3584]{1,0:T(8,128)(2,1)S(1)}, u32[]{:S(2)}, u32[]{:S(2)}) collective-permute-start(bf16[16,3584]{1,0:T(8,128)(2,1)S(1)} %get-tuple-element.48), channel_id=1, source_target_pairs={{2,0},{4,2},{6,4},{8,6},{10,8},{12,10},{14,12},{0,14},{3,1},{5,3},... | collective-permute-start | bytes 344072 | tf_op jit(solution)/shard_map/ppermute | solution.py:335
  101.3 6.8 %collective-permute-start.16 = (bf16[16,3584]{1,0:T(8,128)(2,1)S(1)}, bf16[16,3584]{1,0:T(8,128)(2,1)S(1)}, u32[]{:S(2)}, u32[]{:S(2)}) collective-permute-start(bf16[16,3584]{1,0:T(8,128)(2,1)S(1)} %get-tuple-element.56), channel_id=1, source_target_pairs={{2,0},{4,2},{6,4},{8,6},{10,8},{12,10},{14,12},{0,14},{3,1},{5,3},... | collective-permute-start | bytes 344072 | tf_op jit(solution)/shard_map/ppermute | solution.py:335
  103.1 8.2 %collective-permute-start.13 = (bf16[16,3584]{1,0:T(8,128)(2,1)S(1)}, bf16[16,3584]{1,0:T(8,128)(2,1)S(1)}, u32[]{:S(2)}, u32[]{:S(2)}) collective-permute-start(bf16[16,3584]{1,0:T(8,128)(2,1)S(1)} %get-tuple-element.53), channel_id=1, source_target_pairs={{12,0},{14,2},{0,4},{2,6},{4,8},{6,10},{8,12},{10,14},{13,1},{15,3... | collective-permute-start | bytes 344072 | tf_op jit(solution)/shard_map/ppermute | solution.py:335
  103.3 8.0 %collective-permute-start.14 = (bf16[16,3584]{1,0:T(8,128)(2,1)S(1)}, bf16[16,3584]{1,0:T(8,128)(2,1)S(1)}, u32[]{:S(2)}, u32[]{:S(2)}) collective-permute-start(bf16[16,3584]{1,0:T(8,128)(2,1)S(1)} %get-tuple-element.54), channel_id=1, source_target_pairs={{4,0},{6,2},{8,4},{10,6},{12,8},{14,10},{0,12},{2,14},{5,1},{7,3},... | collective-permute-start | bytes 344072 | tf_op jit(solution)/shard_map/ppermute | solution.py:335
  107.3 6.0 %collective-permute-start.15 = (bf16[16,3584]{1,0:T(8,128)(2,1)S(1)}, bf16[16,3584]{1,0:T(8,128)(2,1)S(1)}, u32[]{:S(2)}, u32[]{:S(2)}) collective-permute-start(bf16[16,3584]{1,0:T(8,128)(2,1)S(1)} %get-tuple-element.55), channel_id=1, source_target_pairs={{14,0},{0,2},{2,4},{4,6},{6,8},{8,10},{10,12},{12,14},{15,1},{1,3}... | collective-permute-start | bytes 344072 | tf_op jit(solution)/shard_map/ppermute | solution.py:335

commit v4 on v3

--- a/solution.py
+++ b/solution.py
@@ -31,26 +31,29 @@
     for group in copies:
         for copy in group:
             copy.start()
-    sent = []
+    scores, sent = [], []
     for r in range(requests):
         for copy in copies[r]:
             copy.wait()
-        keys = cache[r]
-        scores = lax.dot_general(
-            latent[r], keys, (((1,), (1,)), ((), ())), preferred_element_type=jnp.float32
+        score = lax.dot_general(
+            latent[r], cache[r], (((1,), (1,)), ((), ())), preferred_element_type=jnp.float32
         )
-        scores = (
-            scores
+        score = (
+            score
             + lax.dot_general(
                 rope[r], cache_rope[r], (((0,), (0,)), ((), ())), preferred_element_type=jnp.float32
             )
         ) * score_scale
-        position = lax.broadcasted_iota(jnp.int32, scores.shape, 1)
-        scores = jnp.where(position < lengths[r], scores, -1e30)
-        weights = jnp.exp(scores - jnp.max(scores, axis=1, keepdims=True))
-        probabilities = weights / jnp.sum(weights, axis=1, keepdims=True)
+        position = lax.broadcasted_iota(jnp.int32, score.shape, 1)
+        scores.append(jnp.where(position < lengths[r], score, -1e30))
+    weights = [jnp.exp(score - jnp.max(score, axis=1, keepdims=True)) for score in scores]
+    probabilities = [
+        (weight / jnp.sum(weight, axis=1, keepdims=True)).astype(jnp.bfloat16)
+        for weight in weights
+    ]
+    for r in range(requests):
         built[r] = jnp.dot(
-            probabilities.astype(jnp.bfloat16), keys, preferred_element_type=jnp.float32
+            probabilities[r], cache[r], preferred_element_type=jnp.float32
         ).astype(jnp.bfloat16)
         sent.append(pltpu.make_async_copy(built.at[r], out.at[r], out_sems.at[r]))
         sent[-1].start()
@@ -164,27 +167,32 @@
 
 def slots_of(info, experts, count, top):
     gathered, places = info.shape[0], experts.shape[1]
-    names = jnp.zeros((gathered, places), jnp.float32)
-    weight = jnp.zeros((gathered, places), jnp.float32)
-    for k in range(top):
-        match = info[:, k : k + 1] == experts
-        share = (
-            info[:, top + k : top + k + 1]
-            + info[:, 2 * top + k : 2 * top + k + 1]
-            + info[:, 3 * top + k : 3 * top + k + 1]
-        )
-        names = jnp.where(match, 1.0, names)
-        weight = weight + jnp.where(match, share, 0.0)
+    names = info[:, 0:1] == experts
+    for k in range(1, top):
+        names = names | (info[:, k : k + 1] == experts)
     row = lax.broadcasted_iota(jnp.int32, (gathered, gathered), 0)
     column = lax.broadcasted_iota(jnp.int32, (gathered, gathered), 1)
     before = jnp.where((column < row) & (column // count == row // count), 1.0, 0.0)
     rank = jnp.dot(
-        before.astype(jnp.bfloat16), names.astype(jnp.bfloat16), preferred_element_type=jnp.float32
+        before.astype(jnp.bfloat16),
+        jnp.where(names, 1.0, 0.0).astype(jnp.bfloat16),
+        preferred_element_type=jnp.float32,
     )
     token = lax.broadcasted_iota(jnp.int32, (gathered, places), 0)
     slot = lax.broadcasted_iota(jnp.int32, (gathered, places), 1) % (2 * gathered // count)
-    here = (names > 0.0) & ((token // count) * 2 + rank.astype(jnp.int32) == slot)
-    return jnp.where(here, 1.0, 0.0), jnp.where(here, weight, 0.0)
+    return names & ((token // count) * 2 + rank.astype(jnp.int32) == slot)
+
+
+def weights_of(info, experts, top):
+    weight = jnp.zeros((info.shape[0], experts.shape[1]), jnp.float32)
+    shares = (
+        info[:, top : 2 * top] + info[:, 2 * top : 3 * top] + info[:, 3 * top : 4 * top]
+    )
+    for k in range(top):
+        weight = weight + jnp.where(
+            info[:, k : k + 1] == experts, shares[:, k : k + 1], 0.0
+        )
+    return weight
 
 
 def dispatch_kernel(top, own, *refs):
@@ -192,8 +200,8 @@
     count = blocks[0].shape[0]
     width = outgoing.shape[1]
     info = jnp.concatenate([b[:, width:] for b in blocks], axis=0).astype(jnp.float32)
-    place, scale[...] = slots_of(info, own[...], count, top)
-    place = place.astype(jnp.bfloat16)
+    here = slots_of(info, own[...], count, top)
+    place = jnp.where(here, 1.0, 0.0).astype(jnp.bfloat16)
     copies = []
     for i, start in enumerate(range(0, width, STEP)):
         cut = pl.ds(start, STEP)
@@ -203,6 +211,7 @@
         ).astype(jnp.bfloat16)
         copies.append(pltpu.make_async_copy(built.at[:, cut], outgoing.at[:, cut], sems.at[i]))
         copies[-1].start()
+    scale[...] = jnp.where(here, weights_of(info, own[...], top), 0.0)
     for copy in copies:
         copy.wait()
 

time: 115 us -> 114 us (level)
  transfers between devices with their start and end apart: 19 -> 19, of which waited for: 8 -> 9; matrix products, arithmetic and copies ran while one was open for 0% -> 0% of each run, Pallas kernels for 8% -> 7%
where the time goes in v4:
time: 114 us
  starting transfers between devices  34.5 us (30%)
  blocking collectives  33.4 us (29%)
  waiting for transfers between devices  26 us (23%)
  Pallas kernels  19.3 us (17%)
    all_to_all x2, blocking collectives, to_plane(): return lax.all_to_all(x, PLANE, split_axis=0, concat_axis=0, tiled=True)  33.4 us
    ppermute x14, waiting for transfers between devices, from_line(): lax.ppermute(rows, 'z', [((i + distance) % planes, i) for i in range(plan...  25.1 us
    ppermute x14, starting transfers between devices, from_line(): lax.ppermute(rows, 'z', [((i + distance) % planes, i) for i in range(plan...  21.3 us
    all_to_all x2, starting transfers between devices, to_plane(): return lax.all_to_all(x, PLANE, split_axis=0, concat_axis=0, tiled=True)  12.7 us
    pallas_call x1, Pallas kernels, experts(): pl.pallas_call(expert_kernel, out_shape=[pltpu.HBM(half, kind)] * 2, in_s...  9.62 us
    pallas_call x1, Pallas kernels, attention(): pl.pallas_call(attention_kernel, out_shape=pltpu.HBM(query_latent.shape,...  4.06 us
    pallas_call x2, Pallas kernels, dispatch(): pl.pallas_call(functools.partial(dispatch_kernel, top), out_shape=[pltpu....  2.99 us
  transfers between devices with their start and end apart: 19, of which 9 were waited for; matrix products, arithmetic and copies ran while one was open for 0% of the time, Pallas kernels for 7%

profile of v4, /device:TPU:6, one launch (start us, length us, event | category | flops | bytes accessed | tf_op | source)
XLA Modules:
  0.0 114.0 jit_solution(13683106175158374405)
XLA Ops:
  0.6 1.1 shard_map.131.refs_0_
  1.7 6.4 %collective-permute-start = (bf16[16,3712]{1,0:T(8,128)(2,1)S(1)}, bf16[16,3712]{1,0:T(8,128)(2,1)S(1)}, u32[]{:S(2)}, u32[]{:S(2)}) collective-permute-start(bf16[16,3712]{1,0:T(8,128)(2,1)S(1)} %shard_map.131.refs_0_), channel_id=1, source_target_pairs={{4,0},{6,2},{8,4},{10,6},{12,8},{14,10},{0,12},{2,14},{5,1},{7,3},... | collective-permute-start | bytes 356360 | tf_op jit(solution)/shard_map/ppermute | solution.py:344
  8.1 3.7 %collective-permute-start.2 = (bf16[16,3712]{1,0:T(8,128)(2,1)S(1)}, bf16[16,3712]{1,0:T(8,128)(2,1)S(1)}, u32[]{:S(2)}, u32[]{:S(2)}) collective-permute-start(bf16[16,3712]{1,0:T(8,128)(2,1)S(1)} %shard_map.131.refs_0_), channel_id=1, source_target_pairs={{2,0},{4,2},{6,4},{8,6},{10,8},{12,10},{14,12},{0,14},{3,1},{5,3},... | collective-permute-start | bytes 356360 | tf_op jit(solution)/shard_map/ppermute | solution.py:344
  11.8 2.1 %collective-permute-done.refs_2_ = bf16[16,3712]{1,0:T(8,128)(2,1)S(1)} collective-permute-done((bf16[16,3712]{1,0:T(8,128)(2,1)S(1)}, bf16[16,3712]{1,0:T(8,128)(2,1)S(1)}, u32[]{:S(2)}, u32[]{:S(2)}) %collective-permute-start) | collective-permute-done | bytes 118816 | tf_op jit(solution)/shard_map/ppermute | solution.py:344
  14.0 4.0 %collective-permute-done.1.refs_3_ = bf16[16,3712]{1,0:T(8,128)(2,1)S(1)} collective-permute-done((bf16[16,3712]{1,0:T(8,128)(2,1)S(1)}, bf16[16,3712]{1,0:T(8,128)(2,1)S(1)}, u32[]{:S(2)}, u32[]{:S(2)}) %collective-permute-start.1) | collective-permute-done | bytes 118816 | tf_op jit(solution)/shard_map/ppermute | solution.py:344
  18.0 1.6 %collective-permute-done.3.refs_0_ = bf16[16,3712]{1,0:T(8,128)(2,1)S(1)} collective-permute-done((bf16[16,3712]{1,0:T(8,128)(2,1)S(1)}, bf16[16,3712]{1,0:T(8,128)(2,1)S(1)}, u32[]{:S(2)}, u32[]{:S(2)}) %collective-permute-start.3) | collective-permute-done | bytes 118816 | tf_op jit(solution)/shard_map/ppermute | solution.py:344
  20.1 1.5 %shard_map.132 = (bf16[128,3584]{1,0:T(8,128)(2,1)}, f32[64,128]{1,0:T(8,128)S(1)}) custom-call(f32[1,128]{1,0:T(1,128)S(1)} %fusion.2.own, bf16[16,3712]{1,0:T(8,128)(2,1)S(1)} %shard_map.131.refs_0_, bf16[16,3712]{1,0:T(8,128)(2,1)S(1)} %collective-permute-done.2.refs_1_, bf16[16,3712]{1,0:T(8,128)(2,1)S(1)} %collective-permute-done.refs_2_, ...), custom_call_target="tpu_custom_call" | custom-call | flops 58720256 | bytes 1835008 | tf_op jit(solution)/shard_map/pallas_call | solution.py:221
  21.6 7.4 %all-to-all-start = ((bf16[16,8,3584]{2,1,0:T(8,128)(2,1)}), bf16[16,8,3584]{2,1,0:T(8,128)(2,1)S(1)}, u32[]{:S(2)}, u32[]{:S(2)}) async-start(bf16[16,8,3584]{2,1,0:T(8,128)(2,1)} %bitcast.25), calls=%async_computation | async-start | bytes 1835008 | tf_op jit(solution)/shard_map/all_to_all | solution.py:371
  30.3 6.1 %collective-permute-done.4.refs_1_ = bf16[16,3712]{1,0:T(8,128)(2,1)S(1)} collective-permute-done((bf16[16,3712]{1,0:T(8,128)(2,1)S(1)}, bf16[16,3712]{1,0:T(8,128)(2,1)S(1)}, u32[]{:S(2)}, u32[]{:S(2)}) %collective-permute-start.4) | collective-permute-done | bytes 118816 | tf_op jit(solution)/shard_map/ppermute | solution.py:344
  36.4 1.4 %collective-permute-done.5.refs_2_ = bf16[16,3712]{1,0:T(8,128)(2,1)S(1)} collective-permute-done((bf16[16,3712]{1,0:T(8,128)(2,1)S(1)}, bf16[16,3712]{1,0:T(8,128)(2,1)S(1)}, u32[]{:S(2)}, u32[]{:S(2)}) %collective-permute-start.5) | collective-permute-done | bytes 118816 | tf_op jit(solution)/shard_map/ppermute | solution.py:344
  37.8 4.7 %collective-permute-done.6.refs_3_ = bf16[16,3712]{1,0:T(8,128)(2,1)S(1)} collective-permute-done((bf16[16,3712]{1,0:T(8,128)(2,1)S(1)}, bf16[16,3712]{1,0:T(8,128)(2,1)S(1)}, u32[]{:S(2)}, u32[]{:S(2)}) %collective-permute-start.6) | collective-permute-done | bytes 118816 | tf_op jit(solution)/shard_map/ppermute | solution.py:344
  42.4 1.5 %shard_map.133 = (bf16[128,3584]{1,0:T(8,128)(2,1)}, f32[64,128]{1,0:T(8,128)S(1)}) custom-call(f32[1,128]{1,0:T(1,128)S(1)} %fusion.2.own, bf16[16,3712]{1,0:T(8,128)(2,1)S(1)} %collective-permute-done.3.refs_0_, bf16[16,3712]{1,0:T(8,128)(2,1)S(1)} %collective-permute-done.4.refs_1_, bf16[16,3712]{1,0:T(8,128)(2,1)S(1)} %collective-permute-done.5.refs_2_, ...), custom_call_target="tpu_custom_call" | custom-call | flops 58720256 | bytes 1835008 | tf_op jit(solution)/shard_map/pallas_call | solution.py:221
  44.0 17.7 %all_to_all.46 = bf16[16,8,3584]{2,1,0:T(8,128)(2,1)S(1)} all-to-all(bf16[16,8,3584]{2,1,0:T(8,128)(2,1)} %bitcast.26), channel_id=1, replica_groups=mesh['xl'=2,'y'=4,'xh'=2,'z'=8,'c'=2] {'xl','y','xh'}, dimensions={0} | all-to-all | bytes 1835008 | tf_op jit(solution)/shard_map/all_to_all | solution.py:371
  61.7 9.6 %shard_map.134 = (bf16[128,3584]{1,0:T(8,128)(2,1)}, bf16[128,3584]{1,0:T(8,128)(2,1)}) custom-call(bf16[128,3584]{1,0:T(8,128)(2,1)S(1)} %bitcast.16, bf16[128,3584]{1,0:T(8,128)(2,1)S(1)} %bitcast.17, bf16[3584,512]{1,0:T(8,128)(2,1)} %bitcast.19, bf16[3584,512]{1,0:T(8,128)(2,1)} %bitcast.21, bf16[512,3584]{1,0:T(8,128)(2,1)} %bitcast.23, ...), custom_call_target="tpu_custom_call" | custom-call | flops 5637144576 | bytes 22020096 | tf_op jit(solution)/shard_map/pallas_call | solution.py:321
  71.3 15.7 %all_to_all.47 = bf16[16,8,3584]{2,1,0:T(8,128)(2,1)S(1)} all-to-all(bf16[16,8,3584]{2,1,0:T(8,128)(2,1)} %bitcast.27), channel_id=1, replica_groups=mesh['xl'=2,'y'=4,'xh'=2,'z'=8,'c'=2] {'xl','y','xh'}, dimensions={0} | all-to-all | bytes 1835008 | tf_op jit(solution)/shard_map/all_to_all | solution.py:371
  87.1 5.2 %all-to-all-start.3 = ((bf16[16,8,3584]{2,1,0:T(8,128)(2,1)}), bf16[16,8,3584]{2,1,0:T(8,128)(2,1)S(1)}, u32[]{:S(2)}, u32[]{:S(2)}) async-start(bf16[16,8,3584]{2,1,0:T(8,128)(2,1)} %bitcast.24), calls=%async_computation.3 | async-start | bytes 1835008 | tf_op jit(solution)/shard_map/all_to_all | solution.py:371
  93.1 3.1 %collective-permute-start.12 = (bf16[16,3584]{1,0:T(8,128)(2,1)S(1)}, bf16[16,3584]{1,0:T(8,128)(2,1)S(1)}, u32[]{:S(2)}, u32[]{:S(2)}) collective-permute-start(bf16[16,3584]{1,0:T(8,128)(2,1)S(1)} %get-tuple-element.48), channel_id=1, source_target_pairs={{2,0},{4,2},{6,4},{8,6},{10,8},{12,10},{14,12},{0,14},{3,1},{5,3},... | collective-permute-start | bytes 344072 | tf_op jit(solution)/shard_map/ppermute | solution.py:344
  96.3 4.1 %shard_map.136 = bf16[4,128,512]{2,1,0:T(8,128)(2,1)} custom-call(s32[4]{0:T(128)S(1)} %copy-done.1, bf16[4,128,512]{2,1,0:T(8,128)(2,1)} %latent_in.1, bf16[4,64,128]{2,1,0:T(8,128)(2,1)} %bitcast.28, bf16[4,256,512]{2,1,0:T(8,128)(2,1)} %cache_in.1, bf16[4,64,256]{2,1,0:T(8,128)(2,1)} %cache_rope_in.1), custom_call_target="tpu_custom_call" | custom-call | flops 268435456 | bytes 2097152 | tf_op jit(solution)/shard_map/pallas_call | solution.py:68
  100.3 1.4 %collective-permute-start.16 = (bf16[16,3584]{1,0:T(8,128)(2,1)S(1)}, bf16[16,3584]{1,0:T(8,128)(2,1)S(1)}, u32[]{:S(2)}, u32[]{:S(2)}) collective-permute-start(bf16[16,3584]{1,0:T(8,128)(2,1)S(1)} %get-tuple-element.56), channel_id=1, source_target_pairs={{2,0},{4,2},{6,4},{8,6},{10,8},{12,10},{14,12},{0,14},{3,1},{5,3},... | collective-permute-start | bytes 344072 | tf_op jit(solution)/shard_map/ppermute | solution.py:344
  101.7 0.9 all-to-all-done.3
  103.4 3.8 %collective-permute-start.14 = (bf16[16,3584]{1,0:T(8,128)(2,1)S(1)}, bf16[16,3584]{1,0:T(8,128)(2,1)S(1)}, u32[]{:S(2)}, u32[]{:S(2)}) collective-permute-start(bf16[16,3584]{1,0:T(8,128)(2,1)S(1)} %get-tuple-element.54), channel_id=1, source_target_pairs={{4,0},{6,2},{8,4},{10,6},{12,8},{14,10},{0,12},{2,14},{5,1},{7,3},... | collective-permute-start | bytes 344072 | tf_op jit(solution)/shard_map/ppermute | solution.py:344
  107.2 0.8 collective-permute-start.15
  108.1 2.7 %collective-permute-done.13.refs_0_ = bf16[16,3584]{1,0:T(8,128)(2,1)S(1)} collective-permute-done((bf16[16,3584]{1,0:T(8,128)(2,1)S(1)}, bf16[16,3584]{1,0:T(8,128)(2,1)S(1)}, u32[]{:S(2)}, u32[]{:S(2)}) %collective-permute-start.13) | collective-permute-done | bytes 114720 | tf_op jit(solution)/shard_map/ppermute | solution.py:344
  110.8 2.4 %collective-permute-done.15.refs_2_ = bf16[16,3584]{1,0:T(8,128)(2,1)S(1)} collective-permute-done((bf16[16,3584]{1,0:T(8,128)(2,1)S(1)}, bf16[16,3584]{1,0:T(8,128)(2,1)S(1)}, u32[]{:S(2)}, u32[]{:S(2)}) %collective-permute-start.15) | collective-permute-done | bytes 114720 | tf_op jit(solution)/shard_map/ppermute | solution.py:344
  (29 shorter events, 4.1 us)
Async XLA Ops:
  1.7 12.2 %collective-permute-start = (bf16[16,3712]{1,0:T(8,128)(2,1)S(1)}, bf16[16,3712]{1,0:T(8,128)(2,1)S(1)}, u32[]{:S(2)}, u32[]{:S(2)}) collective-permute-start(bf16[16,3712]{1,0:T(8,128)(2,1)S(1)} %shard_map.131.refs_0_), channel_id=1, source_target_pairs={{4,0},{6,2},{8,4},{10,6},{12,8},{14,10},{0,12},{2,14},{5,1},{7,3},... | collective-permute-start | bytes 356360 | tf_op jit(solution)/shard_map/ppermute | solution.py:344
  8.1 9.9 %collective-permute-start.1 = (bf16[16,3712]{1,0:T(8,128)(2,1)S(1)}, bf16[16,3712]{1,0:T(8,128)(2,1)S(1)}, u32[]{:S(2)}, u32[]{:S(2)}) collective-permute-start(bf16[16,3712]{1,0:T(8,128)(2,1)S(1)} %shard_map.131.refs_0_), channel_id=1, source_target_pairs={{12,0},{14,2},{0,4},{2,6},{4,8},{6,10},{8,12},{10,14},{13,1},{15,3... | collective-permute-start | bytes 356360 | tf_op jit(solution)/shard_map/ppermute | solution.py:344
  8.1 9.9 %collective-permute-start.2 = (bf16[16,3712]{1,0:T(8,128)(2,1)S(1)}, bf16[16,3712]{1,0:T(8,128)(2,1)S(1)}, u32[]{:S(2)}, u32[]{:S(2)}) collective-permute-start(bf16[16,3712]{1,0:T(8,128)(2,1)S(1)} %shard_map.131.refs_0_), channel_id=1, source_target_pairs={{2,0},{4,2},{6,4},{8,6},{10,8},{12,10},{14,12},{0,14},{3,1},{5,3},... | collective-permute-start | bytes 356360 | tf_op jit(solution)/shard_map/ppermute | solution.py:344
  11.8 7.8 %collective-permute-start.3 = (bf16[16,3712]{1,0:T(8,128)(2,1)S(1)}, bf16[16,3712]{1,0:T(8,128)(2,1)S(1)}, u32[]{:S(2)}, u32[]{:S(2)}) collective-permute-start(bf16[16,3712]{1,0:T(8,128)(2,1)S(1)} %shard_map.131.refs_0_), channel_id=1, source_target_pairs={{14,0},{0,2},{2,4},{4,6},{6,8},{8,10},{10,12},{12,14},{15,1},{1,3}... | collective-permute-start | bytes 356360 | tf_op jit(solution)/shard_map/ppermute | solution.py:344
  11.8 49.9 %collective-permute-start.7 = (bf16[3584,512]{1,0:T(8,128)(2,1)}, bf16[3584,512]{1,0:T(8,128)(2,1)}, u32[]{:S(2)}, u32[]{:S(2)}) collective-permute-start(bf16[3584,512]{1,0:T(8,128)(2,1)} %bitcast.18), channel_id=1, source_target_pairs={{0,1},{1,0},{2,3},{3,2},{4,5},{5,4},{6,7},{7,6},{8,9},{9,8},{10,11... | collective-permute-start | bytes 11010056 | tf_op jit(solution)/shard_map/ppermute | solution.py:382
  19.6 42.1 %collective-permute-start.8 = (bf16[3584,512]{1,0:T(8,128)(2,1)}, bf16[3584,512]{1,0:T(8,128)(2,1)}, u32[]{:S(2)}, u32[]{:S(2)}) collective-permute-start(bf16[3584,512]{1,0:T(8,128)(2,1)} %bitcast.20), channel_id=1, source_target_pairs={{0,1},{1,0},{2,3},{3,2},{4,5},{5,4},{6,7},{7,6},{8,9},{9,8},{10,11... | collective-permute-start | bytes 11010056 | tf_op jit(solution)/shard_map/ppermute | solution.py:382
  19.6 42.1 %collective-permute-start.9 = (bf16[512,3584]{1,0:T(8,128)(2,1)}, bf16[512,3584]{1,0:T(8,128)(2,1)}, u32[]{:S(2)}, u32[]{:S(2)}) collective-permute-start(bf16[512,3584]{1,0:T(8,128)(2,1)} %bitcast.22), channel_id=1, source_target_pairs={{0,1},{1,0},{2,3},{3,2},{4,5},{5,4},{6,7},{7,6},{8,9},{9,8},{10,11... | collective-permute-start | bytes 11010056 | tf_op jit(solution)/shard_map/ppermute | solution.py:382
  21.6 22.4 %all-to-all-start = ((bf16[16,8,3584]{2,1,0:T(8,128)(2,1)}), bf16[16,8,3584]{2,1,0:T(8,128)(2,1)S(1)}, u32[]{:S(2)}, u32[]{:S(2)}) async-start(bf16[16,8,3584]{2,1,0:T(8,128)(2,1)} %bitcast.25), calls=%async_computation | async-start | bytes 1835008 | tf_op jit(solution)/shard_map/all_to_all | solution.py:371
  29.0 7.4 %collective-permute-start.4 = (bf16[16,3712]{1,0:T(8,128)(2,1)S(1)}, bf16[16,3712]{1,0:T(8,128)(2,1)S(1)}, u32[]{:S(2)}, u32[]{:S(2)}) collective-permute-start(bf16[16,3712]{1,0:T(8,128)(2,1)S(1)} %collective-permute-done.refs_2_), channel_id=1, source_target_pairs={{2,0},{4,2},{6,4},{8,6},{10,8},{12,10},{14,12},{0,14},{3,1},{5,3},... | collective-permute-start | bytes 356360 | tf_op jit(solution)/shard_map/ppermute | solution.py:344
  29.5 8.3 %collective-permute-start.5 = (bf16[16,3712]{1,0:T(8,128)(2,1)S(1)}, bf16[16,3712]{1,0:T(8,128)(2,1)S(1)}, u32[]{:S(2)}, u32[]{:S(2)}) collective-permute-start(bf16[16,3712]{1,0:T(8,128)(2,1)S(1)} %collective-permute-done.refs_2_), channel_id=1, source_target_pairs={{4,0},{6,2},{8,4},{10,6},{12,8},{14,10},{0,12},{2,14},{5,1},{7,3},... | collective-permute-start | bytes 356360 | tf_op jit(solution)/shard_map/ppermute | solution.py:344
  36.4 6.0 %collective-permute-start.6 = (bf16[16,3712]{1,0:T(8,128)(2,1)S(1)}, bf16[16,3712]{1,0:T(8,128)(2,1)S(1)}, u32[]{:S(2)}, u32[]{:S(2)}) collective-permute-start(bf16[16,3712]{1,0:T(8,128)(2,1)S(1)} %collective-permute-done.1.refs_3_), channel_id=1, source_target_pairs={{14,0},{0,2},{2,4},{4,6},{6,8},{8,10},{10,12},{12,14},{15,1},{1,3}... | collective-permute-start | bytes 356360 | tf_op jit(solution)/shard_map/ppermute | solution.py:344
  71.3 24.9 %copy-start.1 = (s32[4]{0:T(128)S(1)}, s32[4]{0:T(128)}, u32[]{:S(2)}) copy-start(s32[4]{0:T(128)} %lengths.1) | copy-start | bytes 52
  71.3 41.9 %copy-start = (bf16[16,3584]{1,0:T(8,128)(2,1)S(1)}, bf16[16,3584]{1,0:T(8,128)(2,1)}, u32[]{:S(2)}) copy-start(bf16[16,3584]{1,0:T(8,128)(2,1)} %tokens.1) | copy-start | bytes 344068
  87.1 15.5 %all-to-all-start.3 = ((bf16[16,8,3584]{2,1,0:T(8,128)(2,1)}), bf16[16,8,3584]{2,1,0:T(8,128)(2,1)S(1)}, u32[]{:S(2)}, u32[]{:S(2)}) async-start(bf16[16,8,3584]{2,1,0:T(8,128)(2,1)} %bitcast.24), calls=%async_computation.3 | async-start | bytes 1835008 | tf_op jit(solution)/shard_map/all_to_all | solution.py:371
  92.7 9.0 %collective-permute-start.10 = (bf16[16,3584]{1,0:T(8,128)(2,1)S(1)}, bf16[16,3584]{1,0:T(8,128)(2,1)S(1)}, u32[]{:S(2)}, u32[]{:S(2)}) collective-permute-start(bf16[16,3584]{1,0:T(8,128)(2,1)S(1)} %get-tuple-element.46), channel_id=1, source_target_pairs={{14,0},{0,2},{2,4},{4,6},{6,8},{8,10},{10,12},{12,14},{15,1},{1,3}... | collective-permute-start | bytes 344072 | tf_op jit(solution)/shard_map/ppermute | solution.py:344
  92.8 8.9 %collective-permute-start.11 = (bf16[16,3584]{1,0:T(8,128)(2,1)S(1)}, bf16[16,3584]{1,0:T(8,128)(2,1)S(1)}, u32[]{:S(2)}, u32[]{:S(2)}) collective-permute-start(bf16[16,3584]{1,0:T(8,128)(2,1)S(1)} %get-tuple-element.47), channel_id=1, source_target_pairs={{12,0},{14,2},{0,4},{2,6},{4,8},{6,10},{8,12},{10,14},{13,1},{15,3... | collective-permute-start | bytes 344072 | tf_op jit(solution)/shard_map/ppermute | solution.py:344
  93.1 8.6 %collective-permute-start.12 = (bf16[16,3584]{1,0:T(8,128)(2,1)S(1)}, bf16[16,3584]{1,0:T(8,128)(2,1)S(1)}, u32[]{:S(2)}, u32[]{:S(2)}) collective-permute-start(bf16[16,3584]{1,0:T(8,128)(2,1)S(1)} %get-tuple-element.48), channel_id=1, source_target_pairs={{2,0},{4,2},{6,4},{8,6},{10,8},{12,10},{14,12},{0,14},{3,1},{5,3},... | collective-permute-start | bytes 344072 | tf_op jit(solution)/shard_map/ppermute | solution.py:344
  100.3 7.7 %collective-permute-start.16 = (bf16[16,3584]{1,0:T(8,128)(2,1)S(1)}, bf16[16,3584]{1,0:T(8,128)(2,1)S(1)}, u32[]{:S(2)}, u32[]{:S(2)}) collective-permute-start(bf16[16,3584]{1,0:T(8,128)(2,1)S(1)} %get-tuple-element.56), channel_id=1, source_target_pairs={{2,0},{4,2},{6,4},{8,6},{10,8},{12,10},{14,12},{0,14},{3,1},{5,3},... | collective-permute-start | bytes 344072 | tf_op jit(solution)/shard_map/ppermute | solution.py:344
  103.0 7.8 %collective-permute-start.13 = (bf16[16,3584]{1,0:T(8,128)(2,1)S(1)}, bf16[16,3584]{1,0:T(8,128)(2,1)S(1)}, u32[]{:S(2)}, u32[]{:S(2)}) collective-permute-start(bf16[16,3584]{1,0:T(8,128)(2,1)S(1)} %get-tuple-element.53), channel_id=1, source_target_pairs={{12,0},{14,2},{0,4},{2,6},{4,8},{6,10},{8,12},{10,14},{13,1},{15,3... | collective-permute-start | bytes 344072 | tf_op jit(solution)/shard_map/ppermute | solution.py:344
  103.4 7.4 %collective-permute-start.14 = (bf16[16,3584]{1,0:T(8,128)(2,1)S(1)}, bf16[16,3584]{1,0:T(8,128)(2,1)S(1)}, u32[]{:S(2)}, u32[]{:S(2)}) collective-permute-start(bf16[16,3584]{1,0:T(8,128)(2,1)S(1)} %get-tuple-element.54), channel_id=1, source_target_pairs={{4,0},{6,2},{8,4},{10,6},{12,8},{14,10},{0,12},{2,14},{5,1},{7,3},... | collective-permute-start | bytes 344072 | tf_op jit(solution)/shard_map/ppermute | solution.py:344
  107.2 6.0 %collective-permute-start.15 = (bf16[16,3584]{1,0:T(8,128)(2,1)S(1)}, bf16[16,3584]{1,0:T(8,128)(2,1)S(1)}, u32[]{:S(2)}, u32[]{:S(2)}) collective-permute-start(bf16[16,3584]{1,0:T(8,128)(2,1)S(1)} %get-tuple-element.55), channel_id=1, source_target_pairs={{14,0},{0,2},{2,4},{4,6},{6,8},{8,10},{10,12},{12,14},{15,1},{1,3}... | collective-permute-start | bytes 344072 | tf_op jit(solution)/shard_map/ppermute | solution.py:344
